TPU v7x, 128 devices: a whole 4x4x4 slice. The times are simulated.
128 devices in a mesh: ctx: 32 (over z, y, core), wsh: 4 (over x).
Axes of the slice: x: 4, y: 4, z: 4, core: 2. Of those that a mesh axis runs over, the one named last changes fastest.
Arguments:
- layer_input: bfloat16 [8, 2048, 1600], P('wsh', 'ctx'), may hold values from -6 to 6
- block_order: int32 [8, 64], P('wsh'), may hold values from 0 to 63, each once within a row
- norm_gains: bfloat16 [2, 1600], P(None, 'wsh'), may hold values from 0.25 to 1.75
- norm_shifts: bfloat16 [2, 1600], P(None, 'wsh'), may hold values from -1.5 to 1.5
- qkv_weight: bfloat16 [1600, 4800], P('wsh'), may hold values from -0.15625 to 0.15625
- attn_bias: bfloat16 [2, 1600], P(None, 'wsh'), may hold values from -2.5 to 2.5
- out_weight: bfloat16 [1600, 1600], P('wsh'), may hold values from -0.625 to 0.625
- out_bias: bfloat16 [1600], P('wsh'), may hold values from -1.5 to 1.5
- fc_weight: bfloat16 [1600, 6400], P('wsh'), may hold values from -0.15625 to 0.15625
- fc_bias: bfloat16 [6400], P('wsh'), may hold values from -2.5 to 2.5
- proj_weight: bfloat16 [6400, 1600], P('wsh'), may hold values from -0.078125 to 0.078125
- proj_bias: bfloat16 [1600], P('wsh'), may hold values from -1.5 to 1.5
- output_grad: bfloat16 [8, 2048, 1600], P('wsh', 'ctx'), may hold values from -6 to 6
Outputs:
- layer_output: bfloat16 [8, 2048, 1600], P('wsh', 'ctx')
- input_grad: float32 [8, 2048, 1600], P('wsh', 'ctx')
- gains_grad: float32 [2, 1600], P(None, 'wsh')
- shifts_grad: float32 [2, 1600], P(None, 'wsh')
- qkv_grad: float32 [1600, 4800], P('wsh')
- attn_bias_grad: float32 [2, 1600], P(None, 'wsh')
- out_weight_grad: float32 [1600, 1600], P('wsh')
- out_bias_grad: float32 [1600], P('wsh')
- fc_weight_grad: float32 [1600, 6400], P('wsh')
- fc_bias_grad: float32 [6400], P('wsh')
- proj_weight_grad: float32 [6400, 1600], P('wsh')
- proj_bias_grad: float32 [1600], P('wsh')
Inputs may be any that keep to these rules, and one draw needn't show every extreme that they name: Each row of block_order names every half-block number of a sequence exactly once.
All inputs are finite; a program needn't handle non-finite values.
Results may differ from a plain program's by a relative error of at most 0.023.
Values may be sent and summed in bfloat16 or wider, within the bound.
No kernel may reach another device: no remote copies, remote signals or barrier semaphores. Data moves between devices by JAX's collectives and lax.ppermute only.
A program may use at most 384 MiB of HBM per device.

v0:
```python
import functools

import jax
import jax.numpy as jnp
from jax import lax
from jax.experimental import pallas as pl
from jax.experimental.pallas import tpu as pltpu
from jax.sharding import Mesh
from jax.sharding import PartitionSpec as P

HEADS = 25
HD = 64
QB = 256
FB = 512
BF = jnp.bfloat16
F32 = jnp.float32
NN = (((1,), (0,)), ((), ()))
NT = (((1,), (1,)), ((), ()))
TN = (((0,), (0,)), ((), ()))
CTX = ("z", "y", "core")


def mm(left, right, dims=NN):
    return lax.dot_general(left, right, dims, preferred_element_type=F32)


def layer_norm(hidden, gain_row, shift_row):
    centered = hidden - jnp.mean(hidden, axis=-1, keepdims=True)
    inverse = lax.rsqrt(jnp.mean(centered * centered, axis=-1, keepdims=True) + 1e-05)
    scaled = centered * inverse
    return scaled * gain_row + shift_row, scaled, inverse


def norm_back(gradient, scaled, inverse, gain_row):
    weighted = gradient * gain_row
    first_mean = jnp.mean(weighted, axis=-1, keepdims=True)
    second_mean = jnp.mean(weighted * scaled, axis=-1, keepdims=True)
    result = inverse * (weighted - first_mean - scaled * second_mean)
    return result, jnp.sum(gradient * scaled, axis=0), jnp.sum(gradient, axis=0)


def gelu_pair(pre_gelu):
    squared = pre_gelu * pre_gelu
    tangent = jnp.tanh(0.7978845608028654 * (pre_gelu + 0.044715 * squared * pre_gelu))
    result = 0.5 * pre_gelu * (1.0 + tangent)
    derivative = 0.5 * (1.0 + tangent) + 0.5 * pre_gelu * (
        1.0 - tangent * tangent
    ) * 0.7978845608028654 * (1.0 + 3.0 * 0.044715 * squared)
    return result, derivative


def ordered_rows(order_ref, seq, block, half, length):
    return pl.multiple_of(seq * length + order_ref[seq, block] * half, half)


def below_mask(size):
    return lax.broadcasted_iota(jnp.int32, (size, size), 0) <= lax.broadcasted_iota(
        jnp.int32, (size, size), 1
    )


def attend_kernel(
    seqs, rows, half, order_ref, in_ref, gain_ref, shift_ref, weight_ref, bias_ref,
    normed_ref, sorted_ref, out_ref, mixed_ref, log_ref, rows_ref,
):
    step = pl.program_id(0)
    tokens = seqs * rows
    group = in_ref.shape[0] // tokens
    length = mixed_ref.shape[2]
    per = rows // half
    normed = layer_norm(in_ref[...].astype(F32), gain_ref[...], shift_ref[...])[0].astype(BF)
    normed_ref[...] = normed
    made = (mm(normed, weight_ref[...], NT) + bias_ref[...]).astype(BF)
    for g in range(group):
        for s in range(seqs):
            for b in range(per):
                at = ordered_rows(order_ref, s, (step * group + g) * per + b, half, length)
                first = g * tokens + s * rows + b * half
                sorted_ref[pl.ds(at, half), :] = made[first : first + half]

    @pl.when(step == pl.num_programs(0) - 1)
    def _():
        below = below_mask(FB)

        def one_seq(s, carry):
            base = pl.multiple_of(s * length, length)
            k_all = sorted_ref[pl.ds(base, length), HD : 2 * HD]
            v_turned = sorted_ref[pl.ds(base, length), 2 * HD :].T
            for i in range(length // FB):
                lo, hi = i * FB, (i + 1) * FB
                q_rows = sorted_ref[pl.ds(base + lo, FB), :HD] * 0.125
                scores = mm(k_all[:hi], q_rows, NT)
                last = jnp.where(below, scores[lo:], -1e30)
                best = jnp.max(last, axis=0, keepdims=True)
                if i:
                    best = jnp.maximum(best, jnp.max(scores[:lo], axis=0, keepdims=True))
                tail = jnp.exp(last - best)
                total = jnp.sum(tail, axis=0, keepdims=True)
                mixed = mm(v_turned[:, lo:hi], tail.astype(BF))
                if i:
                    head = jnp.exp(scores[:lo] - best)
                    total = total + jnp.sum(head, axis=0, keepdims=True)
                    mixed = mixed + mm(v_turned[:, :lo], head.astype(BF))
                mixed = mixed / total
                mixed_ref[s, :, lo:hi] = mixed
                log_ref[s, :, lo:hi] = best + jnp.log(total)
                rows_ref[pl.ds(base + lo, FB), :] = mixed.T
            return carry

        lax.fori_loop(0, seqs, one_seq, 0)

        def one_block(c, carry):
            parts = [
                rows_ref[pl.ds(ordered_rows(order_ref, s, c * per + b, half, length), half), :]
                for s in range(seqs)
                for b in range(per)
            ]
            out_ref[c] = jnp.concatenate(parts, axis=0).T.astype(BF)
            return carry

        lax.fori_loop(0, out_ref.shape[0], one_block, 0)


def attend(order, gathered, gain, shift, weight, bias, rows):
    seqs, halves = order.shape
    tokens, width = seqs * rows, gathered.shape[1]
    n_ctx = gathered.shape[0] // tokens
    length = rows * n_ctx
    half = length // halves
    group = 8
    whole = lambda *shape: pl.BlockSpec(shape, lambda i: (0,) * len(shape))
    return pl.pallas_call(
        functools.partial(attend_kernel, seqs, rows, half),
        grid=(n_ctx // group,),
        in_specs=[
            pl.BlockSpec(memory_space=pltpu.SMEM),
            pl.BlockSpec((group * tokens, width), lambda i: (i, 0)),
            whole(1, width),
            whole(1, width),
            whole(3 * HD, width),
            whole(1, 3 * HD),
        ],
        out_specs=[
            pl.BlockSpec((group * tokens, width), lambda i: (i, 0)),
            whole(seqs * length, 3 * HD),
            whole(n_ctx, HD, tokens),
            whole(seqs, HD, length),
            whole(seqs, 1, length),
        ],
        out_shape=[
            jax.ShapeDtypeStruct(gathered.shape, BF),
            jax.ShapeDtypeStruct((seqs * length, 3 * HD), BF),
            jax.ShapeDtypeStruct((n_ctx, HD, tokens), BF),
            jax.ShapeDtypeStruct((seqs, HD, length), F32),
            jax.ShapeDtypeStruct((seqs, 1, length), F32),
        ],
        scratch_shapes=[pltpu.VMEM((seqs * length, HD), F32)],
        compiler_params=pltpu.CompilerParams(vmem_limit_bytes=48 << 20),
        cost_estimate=pl.CostEstimate(
            flops=20_000_000_000, bytes_accessed=20_000_000, transcendentals=0
        ),
        name="attend",
    )(order, gathered, gain, shift, weight, bias)


def attend_back_kernel(
    seqs, rows, half, order_ref, sorted_ref, mixed_ref, log_ref, grad_ref, out_ref, bias_ref,
    rows_ref, key_ref, value_ref, all_ref,
):
    n_ctx, _, tokens = grad_ref.shape
    length = mixed_ref.shape[2]
    per = rows // half

    def spread(c, carry):
        block = grad_ref[c].T
        for s in range(seqs):
            for b in range(per):
                at = ordered_rows(order_ref, s, c * per + b, half, length)
                first = s * rows + b * half
                rows_ref[pl.ds(at, half), :] = block[first : first + half]
        return carry

    lax.fori_loop(0, n_ctx, spread, 0)
    below = below_mask(QB)

    def one_seq(s, carry):
        base = pl.multiple_of(s * length, length)
        k_all = sorted_ref[pl.ds(base, length), HD : 2 * HD]
        v_all = sorted_ref[pl.ds(base, length), 2 * HD :]
        k_turned = k_all.T
        g_turned = rows_ref[pl.ds(base, length), :].T
        delta = jnp.sum(g_turned.astype(F32) * mixed_ref[s], axis=0, keepdims=True)
        key_ref[...] = jnp.zeros_like(key_ref)
        value_ref[...] = jnp.zeros_like(value_ref)
        for i in range(length // QB):
            lo, hi = i * QB, (i + 1) * QB
            q_rows = sorted_ref[pl.ds(base + lo, QB), :HD] * 0.125
            g_rows = rows_ref[pl.ds(base + lo, QB), :]
            log_row = log_ref[s, :, lo:hi]
            delta_row = delta[:, lo:hi]
            query = jnp.zeros((HD, QB), F32)
            for first, end in ((0, lo), (lo, hi)):
                if first == end:
                    continue
                scores = mm(k_all[first:end], q_rows, NT)
                probs = jnp.exp(scores - log_row)
                if end == hi:
                    probs = jnp.where(below, probs, 0.0)
                slopes = mm(v_all[first:end], g_rows, NT)
                pulled = (probs * (slopes - delta_row)).astype(BF)
                value_ref[first:end, :] += mm(probs.astype(BF), g_rows)
                key_ref[first:end, :] += mm(pulled, q_rows)
                query = query + mm(k_turned[:, first:end], pulled)
            all_ref[pl.ds(base + lo, QB), :HD] = (query * 0.125).T
        all_ref[pl.ds(base, length), HD : 2 * HD] = key_ref[...]
        all_ref[pl.ds(base, length), 2 * HD :] = value_ref[...]
        return carry

    lax.fori_loop(0, seqs, one_seq, 0)

    def one_block(c, carry):
        parts = [
            all_ref[pl.ds(ordered_rows(order_ref, s, c * per + b, half, length), half), :]
            for s in range(seqs)
            for b in range(per)
        ]
        block = jnp.concatenate(parts, axis=0).astype(BF)
        out_ref[c] = block.T
        return carry + jnp.sum(block.astype(F32), axis=0, keepdims=True)

    bias_ref[...] = lax.fori_loop(0, n_ctx, one_block, jnp.zeros((1, 3 * HD), F32))


def attend_back(order, ordered, mixed, logs, grads, rows):
    n_ctx, _, tokens = grads.shape
    seqs, halves = order.shape
    length = rows * n_ctx
    half = length // halves
    vmem = pl.BlockSpec(memory_space=pltpu.VMEM)
    return pl.pallas_call(
        functools.partial(attend_back_kernel, seqs, rows, half),
        in_specs=[pl.BlockSpec(memory_space=pltpu.SMEM)] + [vmem] * 4,
        out_specs=[vmem] * 2,
        out_shape=[
            jax.ShapeDtypeStruct((n_ctx, 3 * HD, tokens), BF),
            jax.ShapeDtypeStruct((1, 3 * HD), F32),
        ],
        scratch_shapes=[
            pltpu.VMEM((seqs * length, HD), BF),
            pltpu.VMEM((length, HD), F32),
            pltpu.VMEM((length, HD), F32),
            pltpu.VMEM((seqs * length, 3 * HD), F32),
        ],
        compiler_params=pltpu.CompilerParams(vmem_limit_bytes=48 << 20),
        cost_estimate=pl.CostEstimate(flops=1, bytes_accessed=1, transcendentals=0),
        name="attend_back",
    )(order, ordered, mixed, logs, grads)


def head_grad_kernel(n_w, at_ref, grad_ref, bias_ref, in_ref, *refs):
    *out_refs, total_ref, turned_ref = refs
    step = pl.program_id(0)

    @pl.when(step == 0)
    def _():
        total_ref[...] = jnp.zeros_like(total_ref)

    turned = jnp.concatenate([grad_ref[g] for g in range(grad_ref.shape[0])], axis=1)
    total_ref[...] += mm(turned, in_ref[...])

    @pl.when(step == pl.num_programs(0) - 1)
    def _():
        turned_ref[...] = total_ref[...].T
        own = turned_ref.shape[0] // n_w
        for k, out_ref in enumerate(out_refs):
            at = pl.multiple_of((at_ref[0] + n_w - k) % n_w * own, 16)
            out_ref[:own] = turned_ref[pl.ds(at, own), :].astype(out_ref.dtype)
            out_ref[own:] = jnp.broadcast_to(
                bias_ref[...], (out_ref.shape[0] - own, out_ref.shape[1])
            ).astype(out_ref.dtype)


def head_grad(at, grads, bias, gathered, n_w):
    n_ctx, _, tokens = grads.shape
    width = gathered.shape[1]
    group = 4
    rows = width // n_w + 16
    return pl.pallas_call(
        functools.partial(head_grad_kernel, n_w),
        grid=(n_ctx // group,),
        in_specs=[
            pl.BlockSpec(memory_space=pltpu.SMEM),
            pl.BlockSpec((group, 3 * HD, tokens), lambda i: (i, 0, 0)),
            pl.BlockSpec((1, 3 * HD), lambda i: (0, 0)),
            pl.BlockSpec((group * tokens, width), lambda i: (i, 0)),
        ],
        out_specs=[pl.BlockSpec((rows, 3 * HD), lambda i: (0, 0))] * n_w,
        out_shape=[
            jax.ShapeDtypeStruct((rows, 3 * HD), BF if k else F32) for k in range(n_w)
        ],
        scratch_shapes=[pltpu.VMEM((3 * HD, width), F32), pltpu.VMEM((width, 3 * HD), F32)],
        compiler_params=pltpu.CompilerParams(vmem_limit_bytes=32 << 20),
        cost_estimate=pl.CostEstimate(flops=1, bytes_accessed=1, transcendentals=0),
        name="head_grad",
    )(at, grads, bias, gathered)


def finish_kernel(n_w, turned_ref, weight_ref, in_ref, gain_ref, shift_ref, middle_ref, side_ref, out_ref, block_ref, total_ref):
    step = pl.program_id(0)

    @pl.when(step == 0)
    def _():
        total_ref[...] = jnp.zeros_like(total_ref)

    total_ref[...] += mm(turned_ref[...].T, weight_ref[...])

    @pl.when(step == pl.num_programs(0) - 1)
    def _():
        grad = total_ref[...]
        _, scaled, inverse = layer_norm(in_ref[...].astype(F32), gain_ref[...], shift_ref[...])
        result, gain_grad, shift_grad = norm_back(grad, scaled, inverse, gain_ref[...])
        out_ref[...] = middle_ref[...] + result
        own = block_ref.shape[2]
        rows = (gain_grad.reshape(1, -1), side_ref[0:1], shift_grad.reshape(1, -1), side_ref[1:2])
        for w in range(n_w):
            at = slice(w * own, (w + 1) * own)
            for r, row in enumerate(rows):
                block_ref[w, r : r + 1] = row[:, at]
            block_ref[w, len(rows) :] = side_ref[2 : 2 + block_ref.shape[1] - len(rows), at]


def finish(turned, weight, low, gain, shift, middle, side, n_w):
    tokens, width = low.shape
    depth = HEADS * 3 * HD // 5
    whole = lambda *shape: pl.BlockSpec(shape, lambda i: (0,) * len(shape))
    return pl.pallas_call(
        functools.partial(finish_kernel, n_w),
        grid=(5,),
        in_specs=[
            pl.BlockSpec((depth, tokens), lambda i: (i, 0)),
            pl.BlockSpec((depth, width), lambda i: (i, 0)),
            whole(tokens, width),
            whole(1, width),
            whole(1, width),
            whole(tokens, width),
            whole(*side.shape),
        ],
        out_specs=[whole(tokens, width), whole(n_w, 8, width // n_w)],
        out_shape=[
            jax.ShapeDtypeStruct((tokens, width), F32),
            jax.ShapeDtypeStruct((n_w, 8, width // n_w), F32),
        ],
        scratch_shapes=[pltpu.VMEM((tokens, width), F32)],
        compiler_params=pltpu.CompilerParams(vmem_limit_bytes=32 << 20),
        cost_estimate=pl.CostEstimate(flops=1, bytes_accessed=1, transcendentals=0),
        name="finish",
    )(turned, weight, low, gain, shift, middle, side)


def join_rows_kernel(n_w, overlap, at_ref, *refs):
    *pieces, out_ref = refs
    wsh, core = at_ref[0], at_ref[1]
    own = pieces[0].shape[0]
    out_ref[pl.ds(pl.multiple_of(wsh * own, 16), own), :] = pieces[0][...]
    for k in range(1, n_w):
        base = (wsh + k) % n_w * own
        mine, other = pieces[2 * k - 1], pieces[2 * k]
        size = mine.shape[0]
        out_ref[pl.ds(pl.multiple_of(base + core * overlap, 16), size), :] = mine[...]
        out_ref[pl.ds(pl.multiple_of(base + (1 - core) * overlap, 16), size), :] = other[...]


def join_rows(at, pieces, n_w, overlap):
    own, width = pieces[0].shape
    vmem = pl.BlockSpec(memory_space=pltpu.VMEM)
    return pl.pallas_call(
        functools.partial(join_rows_kernel, n_w, overlap),
        in_specs=[pl.BlockSpec(memory_space=pltpu.SMEM)] + [vmem] * len(pieces),
        out_specs=vmem,
        out_shape=jax.ShapeDtypeStruct((n_w * own, width), BF),
        compiler_params=pltpu.CompilerParams(vmem_limit_bytes=32 << 20),
        cost_estimate=pl.CostEstimate(flops=1, bytes_accessed=1, transcendentals=0),
        name="join_rows",
    )(at, *pieces)


def cut_columns_kernel(n_w, overlap, at_ref, in_ref, *out_refs):
    wsh, core = at_ref[0], at_ref[1]
    cols = out_refs[0].shape[1]
    for k, out_ref in enumerate(out_refs):
        size = out_ref.shape[0]
        start = 0 if k == 0 else pl.multiple_of(core * overlap, 16)
        for b in range(n_w):

            @pl.when((wsh + n_w - k) % n_w == b)
            def _(out_ref=out_ref, start=start, size=size, b=b):
                out_ref[...] = in_ref[pl.ds(start, size), b * cols : (b + 1) * cols]


def cut_columns(at, array, n_w, size, overlap):
    own, cols = array.shape[0], array.shape[1] // n_w
    vmem = pl.BlockSpec(memory_space=pltpu.VMEM)
    return pl.pallas_call(
        functools.partial(cut_columns_kernel, n_w, overlap),
        in_specs=[pl.BlockSpec(memory_space=pltpu.SMEM), vmem],
        out_specs=[vmem] * n_w,
        out_shape=[
            jax.ShapeDtypeStruct((own if k == 0 else size, cols), BF) for k in range(n_w)
        ],
        compiler_params=pltpu.CompilerParams(vmem_limit_bytes=32 << 20),
        cost_estimate=pl.CostEstimate(flops=1, bytes_accessed=1, transcendentals=0),
        name="cut_columns",
    )(at, array)


def join_columns_kernel(n_w, overlap, at_ref, *refs):
    *pieces, out_ref = refs
    wsh, core = at_ref[0], at_ref[1]
    cols = pieces[0].shape[1]
    for k in range(n_w):
        for b in range(n_w):

            @pl.when((wsh + k) % n_w == b)
            def _(k=k, b=b):
                at = slice(b * cols, (b + 1) * cols)
                if k == 0:
                    out_ref[:, at] = pieces[0][...].astype(F32)
                    return
                mine, other = pieces[2 * k - 1], pieces[2 * k]
                size = mine.shape[0]
                out_ref[pl.ds(pl.multiple_of(core * overlap, 16), size), at] = mine[...].astype(F32)
                out_ref[pl.ds(pl.multiple_of((1 - core) * overlap, 16), size), at] = other[
                    ...
                ].astype(F32)


def join_columns(at, pieces, n_w, overlap):
    own, cols = pieces[0].shape
    vmem = pl.BlockSpec(memory_space=pltpu.VMEM)
    return pl.pallas_call(
        functools.partial(join_columns_kernel, n_w, overlap),
        in_specs=[pl.BlockSpec(memory_space=pltpu.SMEM)] + [vmem] * len(pieces),
        out_specs=vmem,
        out_shape=jax.ShapeDtypeStruct((own, n_w * cols), F32),
        compiler_params=pltpu.CompilerParams(vmem_limit_bytes=40 << 20),
        cost_estimate=pl.CostEstimate(flops=1, bytes_accessed=1, transcendentals=0),
        name="join_columns",
    )(at, *pieces)


def out_grad_kernel(n_w, in_ref, grad_ref, side_ref, out_ref):
    made = mm(in_ref[...], grad_ref[...])
    chunks = made.shape[0] // 16
    out_ref[...] = jnp.zeros_like(out_ref)
    for c in range(chunks):
        out_ref[c] = made[c * 16 : (c + 1) * 16].astype(BF)
    out_ref[chunks, :1] = side_ref[...].astype(BF)


def out_grad(rows, grads, side, n_ctx, n_w):
    vmem = pl.BlockSpec(memory_space=pltpu.VMEM)
    return pl.pallas_call(
        functools.partial(out_grad_kernel, n_w),
        in_specs=[vmem] * 3,
        out_specs=vmem,
        out_shape=jax.ShapeDtypeStruct((n_ctx, 16, grads.shape[1]), BF),
        compiler_params=pltpu.CompilerParams(vmem_limit_bytes=24 << 20),
        cost_estimate=pl.CostEstimate(flops=1, bytes_accessed=1, transcendentals=0),
        name="out_grad",
    )(rows, grads, side)


def pack_kernel(chunk_ref, *refs):
    *pieces, left_ref, right_ref = refs
    total = pieces[0][...]
    for piece in pieces[1:]:
        total = total + piece[...].astype(F32)
    left_ref[...] = total[:, : 2 * HD].astype(BF)
    chunk = chunk_ref[0].astype(F32)
    for c in range(1, chunk_ref.shape[0]):
        chunk = chunk + chunk_ref[c].astype(F32)
    turned = jnp.concatenate(
        [chunk[:, q * HD : (q + 1) * HD] for q in range(chunk.shape[1] // HD)], axis=0
    )
    turned = jnp.concatenate(
        [turned, jnp.zeros((total.shape[0] - turned.shape[0], HD), F32)], axis=0
    )
    right_ref[...] = jnp.concatenate([total[:, 2 * HD :], turned], axis=1).astype(BF)


def pack(chunks, pieces):
    rows = pieces[0].shape[0]
    vmem = pl.BlockSpec(memory_space=pltpu.VMEM)
    return pl.pallas_call(
        pack_kernel,
        in_specs=[vmem] * (1 + len(pieces)),
        out_specs=[vmem] * 2,
        out_shape=[jax.ShapeDtypeStruct((rows, 2 * HD), BF)] * 2,
        compiler_params=pltpu.CompilerParams(vmem_limit_bytes=24 << 20),
        cost_estimate=pl.CostEstimate(flops=1, bytes_accessed=1, transcendentals=0),
        name="pack",
    )(chunks, *pieces)


def unpack_kernel(
    at_ref, left_own, left_other, right_own, right_other, qkv_ref, out_ref, bias_ref, side_ref
):
    z, y, core = at_ref[0], at_ref[1], at_ref[2]
    own = qkv_ref.shape[0]
    bias_ref[...] = jnp.zeros_like(bias_ref)
    for h in range(HEADS + 1):
        by_z, by_y = (h // 8 + 4 - z) % 4, ((h // 2) % 4 + 4 - y) % 4
        same = core == h % 2
        right_at = by_y * 4 + by_z
        right = jnp.where(same, right_own[right_at], right_other[right_at]).astype(F32)
        if h == HEADS:
            for q in range(HEADS):
                side_ref[:, q * HD : (q + 1) * HD] = right[q * 16 : q * 16 + 8, HD:]
            break
        left_at = by_z * 4 + by_y
        left = jnp.where(same, left_own[left_at], left_other[left_at]).astype(F32)
        for part, piece in enumerate((left[:, :HD], left[:, HD:], right[:, :HD])):
            at = (part * HEADS + h) * HD
            qkv_ref[:, at : at + HD] = piece[:own]
        bias_ref[0:1, h * HD : (h + 1) * HD] = left[own : own + 1, :HD]
        bias_ref[1:2, h * HD : (h + 1) * HD] = right[own : own + 1, :HD]
        for q in range(HEADS):
            out_ref[h * 16 : (h + 1) * 16, q * HD : (q + 1) * HD] = right[
                q * 16 : (q + 1) * 16, HD:
            ]


def unpack(at, left_own, left_other, right_own, right_other):
    rows = left_own.shape[1] - 16
    vmem = pl.BlockSpec(memory_space=pltpu.VMEM)
    return pl.pallas_call(
        unpack_kernel,
        in_specs=[pl.BlockSpec(memory_space=pltpu.SMEM)] + [vmem] * 4,
        out_specs=[vmem] * 4,
        out_shape=[
            jax.ShapeDtypeStruct((rows, 3 * HEADS * HD), F32),
            jax.ShapeDtypeStruct((rows, HEADS * HD), F32),
            jax.ShapeDtypeStruct((8, HEADS * HD), F32),
            jax.ShapeDtypeStruct((8, HEADS * HD), F32),
        ],
        compiler_params=pltpu.CompilerParams(vmem_limit_bytes=40 << 20),
        cost_estimate=pl.CostEstimate(flops=1, bytes_accessed=1, transcendentals=0),
        name="unpack",
    )(at, left_own, left_other, right_own, right_other)


def after(array, *others):
    return lax.optimization_barrier((array, *others))[0]


def on_device(
    layer_input,
    block_order,
    norm_gains,
    norm_shifts,
    qkv_weight,
    attn_bias,
    out_weight,
    out_bias,
    fc_weight,
    fc_bias,
    proj_weight,
    proj_bias,
    output_grad,
):
    seqs, rows, width = layer_input.shape
    tokens = seqs * rows
    n_ctx, n_w = lax.axis_size(CTX), lax.axis_size("wsh")
    ctx, wsh = lax.axis_index(CTX), lax.axis_index("wsh")
    z, y, core = (lax.axis_index(axis) for axis in CTX)
    own = width // n_w
    ff = fc_weight.shape[1] // n_w
    size, overlap = 208, 192
    at_x = jnp.stack([wsh, core])

    def shift(array, axis, k):
        size = lax.axis_size(axis)
        return lax.ppermute(array, axis, [((i + k) % size, i) for i in range(size)])

    def x_shift(array, k):
        return shift(array, "wsh", k)

    def partner(array):
        return shift(array, "core", 1)

    def around(array):
        return [array] + [x_shift(array, k) for k in range(1, n_w)]

    def deal(choose):
        return [choose(0)] + [x_shift(choose(k), k) for k in range(1, n_w)]

    def with_halves(whole, halves, *before):
        pieces = [whole]
        for k in range(1, n_w):
            mine = x_shift(halves[k - 1], k)
            pieces += [mine, partner(after(mine, *before))]
        return pieces

    def in_order(pieces):
        twice = jnp.stack(pieces + pieces)
        start = (n_w - wsh) % n_w
        return lax.dynamic_slice(twice, (start,) + (0,) * pieces[0].ndim, (n_w,) + pieces[0].shape)

    low = layer_input.reshape(tokens, width)
    gathered = lax.all_gather(low, CTX, axis=0, tiled=True)
    packed = jnp.concatenate(
        [norm_gains, norm_shifts, attn_bias, out_bias[None], proj_bias[None]], axis=0
    )
    vectors = in_order(around(packed)).transpose(1, 0, 2).reshape(8, width).astype(F32)
    gains, shifts, bias_pair = vectors[0:2], vectors[2:4], vectors[4:6]
    out_bias_row, proj_bias_row = vectors[6], vectors[7]

    head = jnp.minimum(ctx, HEADS - 1)
    head_cols = jnp.concatenate(
        [
            lax.dynamic_slice(qkv_weight, (0, part * width + head * HD), (own, HD))
            for part in range(3)
        ],
        axis=1,
    )
    head_weight = in_order(around(head_cols)).reshape(width, 3 * HD).T
    head_bias = lax.dynamic_slice(bias_pair, (0, head * HD), (2, HD))
    head_bias = jnp.concatenate([head_bias[:1], jnp.zeros((1, HD), F32), head_bias[1:]], axis=1)

    grad_low = output_grad.reshape(tokens, width)
    out_half = lax.dynamic_slice(
        after(out_weight, head_weight), (core * overlap, 0), (size, width)
    )
    out_pieces = with_halves(out_weight, [out_half] * (n_w - 1))
    out_all = join_rows(at_x, out_pieces, n_w, overlap)
    fc_own, *fc_halves = cut_columns(at_x, fc_weight, n_w, size, overlap)
    fc_halves = [after(half, *out_pieces[1::2]) for half in fc_halves]
    gathered = after(gathered, out_all)

    input_one, ordered, mixed_turned, mixed, logs = attend(
        block_order, gathered, gains[:1], shifts[:1], head_weight, head_bias, rows
    )
    grad_group = jnp.concatenate(around(after(grad_low, mixed_turned)), axis=0)
    grad_active = mm(grad_group, proj_weight, NT)
    fc_pieces = with_halves(fc_own, fc_halves, mixed_turned)
    mixed_turned = after(mixed_turned, *fc_pieces[1::2])
    attended = lax.all_to_all(mixed_turned, CTX, 0, 0).reshape(n_ctx * HD, tokens)[:width]
    attended = after(attended, grad_group, *fc_pieces)
    fc_cols = join_rows(at_x, [after(fc_pieces[0], attended), *fc_pieces[1:]], n_w, overlap)
    residual = low.astype(F32)
    middle = residual + mm(attended, out_all, TN) + out_bias_row
    normed_two, scaled_two, inverse_two = layer_norm(middle, gains[1], shifts[1])
    normed_two = normed_two.astype(BF)
    weight_all = lax.all_gather(head_weight, CTX, axis=0, tiled=True)
    input_two = around(normed_two)
    *input_two, grad_active = lax.optimization_barrier((*input_two, grad_active))
    input_two = jnp.concatenate(input_two, axis=0)

    pre_gelu = mm(input_two, fc_cols) + fc_bias.astype(F32)
    activated, derivative = gelu_pair(pre_gelu)
    activated = activated.astype(BF)
    grad_pre = (grad_active * derivative).astype(BF)
    grad_two = mm(grad_pre, fc_cols, NT).reshape(n_w, tokens, width)
    parts = [grad_two[k].astype(BF) for k in range(1, n_w)]
    activated, grad_pre, *parts = lax.optimization_barrier((activated, grad_pre, *parts))
    came = [x_shift(part, n_w - k) for k, part in enumerate(parts, 1)]
    grad_proj = mm(activated, grad_group, TN).astype(BF)
    grad_fc = mm(input_two, grad_pre, TN).astype(BF)
    branch = mm(after(activated, came[0]), proj_weight).reshape(n_w, tokens, width)
    branch_own, branch_parts = branch[0], [branch[k].astype(BF) for k in range(1, n_w)]
    *came, branch_own = lax.optimization_barrier(
        (*came, branch_own, *branch_parts, grad_proj, grad_fc, weight_all)
    )[:n_w]
    grad_two = grad_two[0] + sum(piece.astype(F32) for piece in came)
    grad_fc_bias = jnp.sum(grad_pre.astype(F32), axis=0, keepdims=True)
    share_proj, share_fc = lax.psum((grad_proj, grad_fc), CTX)

    grad_norm_two, gain_two, shift_two = norm_back(grad_two, scaled_two, inverse_two, gains[1])
    grad_middle = grad_low.astype(F32) + grad_norm_two
    grad_branch = grad_middle.astype(BF)
    grad_attended = mm(out_all, grad_branch, NT).astype(BF)
    grad_heads = jnp.pad(grad_attended, ((0, (n_ctx - HEADS) * HD), (0, 0)))
    grad_heads = lax.all_to_all(grad_heads.reshape(n_ctx, HD, tokens), CTX, 0, 0)
    branch_group = jnp.concatenate(around(after(grad_branch, grad_attended)), axis=0)
    attended_rows = jnp.concatenate(
        deal(
            lambda k: lax.dynamic_slice(
                after(attended, came[0]), ((wsh + n_w - k) % n_w * own, 0), (own, tokens)
            )
        ),
        axis=1,
    )

    branch_came = [
        x_shift(after(part, branch_group), n_w - k) for k, part in enumerate(branch_parts, 1)
    ]
    branch = branch_own + sum(piece.astype(F32) for piece in branch_came)
    layer_output = (middle + branch + proj_bias_row).astype(BF)

    chunks = out_grad(attended_rows, branch_group, grad_fc_bias, n_ctx, n_w)
    grad_heads = after(grad_heads, chunks)
    chunks = lax.all_to_all(chunks, CTX, 0, 0)

    grad_qkv, grad_bias = attend_back(block_order, ordered, mixed, logs, grad_heads, rows)
    grad_tokens = lax.all_to_all(grad_qkv, CTX, 0, 0).reshape(n_ctx * 3 * HD, tokens)

    dealt = head_grad(at_x, grad_qkv, grad_bias, after(input_one, *branch_came), n_w)
    pieces = deal(lambda k: dealt[k])
    left, right = pack(chunks, pieces)
    left = jnp.stack([left] + [shift(left, "y", k) for k in range(1, 4)])
    right = jnp.stack([right] + [shift(right, "z", k) for k in range(1, 4)])
    left = jnp.concatenate([left] + [shift(left, "z", k) for k in range(1, 4)])
    right = jnp.concatenate([right] + [shift(right, "y", k) for k in range(1, 4)])
    side = jnp.stack(
        [
            gain_two,
            shift_two,
            jnp.sum(grad_low.astype(F32), axis=0),
            jnp.sum(grad_branch.astype(F32), axis=0),
        ]
    )
    side = jnp.pad(side, ((0, 4), (0, 0)))
    input_grad, blocks = finish(
        grad_tokens, weight_all, low, gains[:1], shifts[:1], grad_middle, side, n_w
    )
    pieces = deal(
        lambda k: lax.dynamic_slice(blocks, ((wsh + n_w - k) % n_w, 0, 0), (1, 8, own))
    )
    vector_sum = (pieces[0] + pieces[1]) + (pieces[2] + pieces[3])
    everyone = lax.all_to_all(jnp.broadcast_to(vector_sum, (n_ctx, 8, own)), CTX, 0, 0)
    vector_out = jnp.sum(everyone, axis=0)

    qkv_out, out_out, bias_out, side_out = unpack(
        jnp.stack([z, y, core]), after(left, blocks), partner(left), right, partner(right)
    )
    bias_out = lax.dynamic_slice(bias_out, (0, wsh * own), (2, own))

    proj_out = share_proj.astype(F32)
    rows_for = lambda k, start, count: lax.dynamic_slice(
        share_fc, ((wsh + n_w - k) % n_w * own + start, 0), (count, ff)
    )
    fc_out = join_columns(
        at_x,
        with_halves(
            rows_for(0, 0, own),
            [rows_for(k, core * overlap, size) for k in range(1, n_w)],
            qkv_out,
            proj_out,
        ),
        n_w,
        overlap,
    )
    return (
        layer_output.reshape(seqs, rows, width),
        input_grad.reshape(seqs, rows, width),
        vector_out[0:2],
        vector_out[2:4],
        qkv_out,
        bias_out,
        out_out,
        vector_out[5],
        fc_out,
        side_out[0],
        proj_out,
        vector_out[4],
    )


def solution(mesh):
    y, core = 4, 2
    split = Mesh(
        mesh.devices.reshape(mesh.shape["ctx"] // (y * core), y, core, mesh.shape["wsh"]),
        (*CTX, "wsh"),
    )
    return jax.shard_map(
        on_device,
        mesh=split,
        in_specs=(
            P("wsh", CTX, None),
            P("wsh", None),
            P(None, "wsh"),
            P(None, "wsh"),
            P("wsh", None),
            P(None, "wsh"),
            P("wsh", None),
            P("wsh"),
            P("wsh", None),
            P("wsh"),
            P("wsh", None),
            P("wsh"),
            P("wsh", CTX, None),
        ),
        out_specs=(
            P("wsh", CTX, None),
            P("wsh", CTX, None),
            P(None, "wsh"),
            P(None, "wsh"),
            P("wsh", None),
            P(None, "wsh"),
            P("wsh", None),
            P("wsh"),
            P("wsh", None),
            P("wsh"),
            P("wsh", None),
            P("wsh"),
        ),
        check_vma=False,
    )
```

profile of v0, /device:TPU:1, one launch (start us, length us, event | category | flops | bytes accessed | tf_op | source)
XLA Modules:
  0.0 463.2 jit_solution(6528982884569411263)
XLA Ops:
  9.3 3.4 collective-permute-start
  13.8 3.8 collective-permute-done
  19.8 5.7 %collective-permute-done.2 = bf16[400,192]{1,0:T(8,128)(2,1)S(1)} collective-permute-done((bf16[400,192]{1,0:T(8,128)(2,1)S(1)}, bf16[400,192]{1,0:T(8,128)(2,1)S(1)}, u32[]{:S(2)}, u32[]{:S(2)}) %collective-permute-start.2) | collective-permute-done | bytes 153632 | tf_op jit(solution)/shard_map/ppermute | solution.py:583
  39.8 12.8 %collective-permute-done.3.refs_1_ = bf16[208,1600]{1,0:T(8,128)(2,1)} collective-permute-done((bf16[208,1600]{1,0:T(8,128)(2,1)S(1)}, bf16[208,1600]{1,0:T(8,128)(2,1)}, u32[]{:S(2)}, u32[]{:S(2)}) %collective-permute-start.3) | collective-permute-done | bytes 665632 | tf_op jit(solution)/shard_map/ppermute | solution.py:583
  52.6 15.8 %collective-permute-start.4 = (bf16[208,1600]{1,0:T(8,128)(2,1)}, bf16[208,1600]{1,0:T(8,128)(2,1)}, u32[]{:S(2)}, u32[]{:S(2)}) collective-permute-start(bf16[208,1600]{1,0:T(8,128)(2,1)} %collective-permute-done.3.refs_1_), channel_id=1, source_target_pairs={{4,0},{0,4},{5,1},{1,5},{6,2},{2,6},{7,3},{3,7},{12,8},{8,12},{13,... | collective-permute-start | bytes 1996808 | tf_op jit(solution)/shard_map/ppermute | solution.py:583
  68.4 3.3 collective-permute-done.7.refs_5_
  75.0 2.6 join_rows.2
  80.0 26.9 %attend.1 = (bf16[4096,1600]{1,0:T(8,128)(2,1)}, bf16[4096,192]{1,0:T(8,128)(2,1)S(1)}, bf16[32,64,128]{2,1,0:T(8,128)(2,1)}, f32[2,64,2048]{2,1,0:T(8,128)S(1)}, f32[2,1,2048]{2,1,0:T(1,128)S(1)}) custom-call(s32[2,64]{1,0:T(2,128)S(1)} %copy-done.14, bf16[4096,1600]{1,0:T(8,128)(2,1)} %all-gather.3.cloned.1.call-done.in_ref, ...), custom_call_target="tpu_custom_call" | custom-call | flops 20000000000 | bytes 20000000 | tf_op jit(solution)/shard_map/attend/pallas_call | solution.py:132
  113.3 10.0 %all-to-all-start = ((bf16[32,64,128]{2,1,0:T(8,128)(2,1)}), bf16[32,64,128]{2,1,0:T(8,128)(2,1)}, u32[]{:S(2)}, u32[]{:S(2)}) async-start(bf16[32,64,128]{2,1,0:T(8,128)(2,1)} %get-tuple-element.82), calls=%async_computation | async-start | bytes 1048576 | tf_op jit(solution)/shard_map/all_to_all | solution.py:647
  125.8 5.1 %collective-permute-start.20 = (bf16[208,1600]{1,0:T(8,128)(2,1)}, bf16[208,1600]{1,0:T(8,128)(2,1)}, u32[]{:S(2)}, u32[]{:S(2)}) collective-permute-start(bf16[208,1600]{1,0:T(8,128)(2,1)} %collective-permute-done.14.refs_5_), channel_id=1, source_target_pairs={{4,0},{0,4},{5,1},{1,5},{6,2},{2,6},{7,3},{3,7},{12,8},{8,12},{13,... | collective-permute-start | bytes 1996808 | tf_op jit(solution)/shard_map/ppermute | solution.py:583
  136.3 3.0 all-to-all-done
  140.4 4.1 fusion.8
  148.6 5.8 %fusion.11 = f32[512,1600]{0,1:T(8,128)S(1)} fusion(bf16[512,1600]{1,0:T(8,128)(2,1)} %constant_dynamic-update-slice_fusion.8, bf16[1600,1600]{1,0:T(8,128)(2,1)} %param.23), kind=kOutput, calls=%fused_computation.115 | convolution fusion | flops 2621440000 | bytes 10035200 | tf_op jit(solution)/shard_map/dot_general | solution.py:24
  157.4 12.0 %collective-permute-done.23 = bf16[128,1600]{1,0:T(8,128)(2,1)S(1)} collective-permute-done((bf16[128,1600]{1,0:T(8,128)(2,1)S(1)}, bf16[128,1600]{1,0:T(8,128)(2,1)S(1)}, u32[]{:S(2)}, u32[]{:S(2)}) %collective-permute-start.23) | collective-permute-done | bytes 409632 | tf_op jit(solution)/shard_map/ppermute | solution.py:583
  169.6 3.2 convolution_add_fusion
  175.1 5.3 %fusion.9 = (bf16[512,1600]{1,0:T(8,128)(2,1)S(1)}, f32[512,1600]{1,0:T(8,128)}) fusion(bf16[512,1600]{0,1:T(8,128)(2,1)S(1)} %get-tuple-element.100, bf16[1600,1600]{1,0:T(8,128)(2,1)S(1)} %join_rows.3), kind=kOutput, calls=%fused_computation.113 | convolution fusion | flops 2622259200 | bytes 11673600 | tf_op jit(solution)/shard_map/dot_general | solution.py:24
  185.4 5.7 %convolution_convert_fusion = bf16[1600,1600]{1,0:T(8,128)(2,1)} fusion(bf16[512,1600]{1,0:T(8,128)(2,1)S(1)} %constant_dynamic-update-slice_fusion.12, bf16[512,1600]{0,1:T(8,128)(2,1)S(1)} %get-tuple-element.100), kind=kOutput, calls=%fused_computation | convolution fusion | flops 2624000000 | bytes 8396800 | tf_op jit(solution)/shard_map/dot_general | solution.py:24
  191.1 6.3 %convolution_convert_fusion.1 = bf16[1600,1600]{1,0:T(8,128)(2,1)} fusion(bf16[512,1600]{0,1:T(8,128)(2,1)S(1)} %get-tuple-element.99, bf16[512,1600]{1,0:T(8,128)(2,1)} %constant_dynamic-update-slice_fusion.8), kind=kOutput, calls=%fused_computation.1 | convolution fusion | flops 2624000000 | bytes 8396800 | tf_op jit(solution)/shard_map/dot_general | solution.py:24
  197.4 5.2 %collective-permute-done.24 = bf16[128,1600]{1,0:T(8,128)(2,1)S(1)} collective-permute-done((bf16[128,1600]{1,0:T(8,128)(2,1)S(1)}, bf16[128,1600]{1,0:T(8,128)(2,1)S(1)}, u32[]{:S(2)}, u32[]{:S(2)}) %collective-permute-start.24) | collective-permute-done | bytes 409632 | tf_op jit(solution)/shard_map/ppermute | solution.py:583
  202.6 6.1 %fusion.10 = (bf16[512,1600]{1,0:T(8,128)(2,1)S(1)}, f32[512,1600]{1,0:T(8,128)S(1)}) fusion(bf16[512,1600]{0,1:T(8,128)(2,1)S(1)} %get-tuple-element.99, bf16[1600,1600]{1,0:T(8,128)(2,1)} %param.23), kind=kOutput, calls=%fused_computation.114 | convolution fusion | flops 2622259200 | bytes 11673600 | tf_op jit(solution)/shard_map/dot_general | solution.py:24
  215.8 4.2 convolution_convert_fusion.2
  222.2 3.7 collective-permute-start.34
  227.9 9.5 %all-to-all-start.1 = ((bf16[32,64,128]{2,1,0:T(8,128)(2,1)}), bf16[32,64,128]{2,1,0:T(8,128)(2,1)S(1)}, u32[]{:S(2)}, u32[]{:S(2)}) async-start(bf16[32,64,128]{2,1,0:T(8,128)(2,1)} %bitcast.17), calls=%async_computation.1 | async-start | bytes 1048576 | tf_op jit(solution)/shard_map/all_to_all | solution.py:683
  239.1 4.8 %collective-permute-done.33 = bf16[400,128]{1,0:T(8,128)(2,1)S(1)} collective-permute-done((bf16[400,128]{1,0:T(8,128)(2,1)S(1)}, bf16[400,128]{1,0:T(8,128)(2,1)S(1)}, u32[]{:S(2)}, u32[]{:S(2)}) %collective-permute-start.33) | collective-permute-done | bytes 102432 | tf_op jit(solution)/shard_map/ppermute | solution.py:583
  245.1 5.1 %collective-permute-done.29 = bf16[128,1600]{1,0:T(8,128)(2,1)S(1)} collective-permute-done((bf16[128,1600]{1,0:T(8,128)(2,1)}, bf16[128,1600]{1,0:T(8,128)(2,1)S(1)}, u32[]{:S(2)}, u32[]{:S(2)}) %collective-permute-start.29) | collective-permute-done | bytes 409632 | tf_op jit(solution)/shard_map/ppermute | solution.py:583
  252.3 8.1 %all-to-all-start.4 = ((bf16[32,16,1600]{2,1,0:T(8,128)(2,1)}), bf16[32,16,1600]{2,1,0:T(8,128)(2,1)S(1)}, u32[]{:S(2)}, u32[]{:S(2)}) async-start(bf16[32,16,1600]{2,1,0:T(8,128)(2,1)} %out_grad.1), calls=%async_computation.4 | async-start | bytes 3407872 | tf_op jit(solution)/shard_map/all_to_all | solution.py:702
  264.4 21.2 %attend_back.1 = (bf16[32,192,128]{2,1,0:T(8,128)(2,1)}, f32[1,192]{1,0:T(1,128)S(1)}) custom-call(s32[2,64]{1,0:T(2,128)S(1)} %copy-done.14, bf16[4096,192]{1,0:T(8,128)(2,1)S(1)} %copy-done.9, f32[2,64,2048]{2,1,0:T(8,128)S(1)} %copy-done.11, f32[2,1,2048]{2,1,0:T(1,128)S(1)} %get-tuple-element.111.log_ref, bf16[32,64,128]{2,1,0:T(8,128)(2,1)S(1)} %all-to-all-done.1.grad_ref), custom_call_target="tpu_custom_call" | custom-call | flops 1 | bytes 1 | tf_op jit(solution)/shard_map/attend_back/pallas_call | solution.py:240
  285.7 5.5 %copy-done.1 = bf16[4096,1600]{1,0:T(8,128)(2,1)S(1)} copy-done((bf16[4096,1600]{1,0:T(8,128)(2,1)S(1)}, bf16[4096,1600]{1,0:T(8,128)(2,1)}, u32[]{:S(2)}) %copy-start.1) | copy-done | bytes 13107224
  291.2 8.1 %head_grad.1 = (f32[416,192]{1,0:T(8,128)S(1)}, bf16[416,192]{1,0:T(8,128)(2,1)}, bf16[416,192]{1,0:T(8,128)(2,1)}, bf16[416,192]{1,0:T(8,128)(2,1)}) custom-call(s32[2]{0:T(128)S(1)} %pad_add_fusion.at_ref, bf16[32,192,128]{2,1,0:T(8,128)(2,1)} %get-tuple-element.114.grad_ref, f32[1,192]{1,0:T(1,128)S(1)} %get-tuple-element.117.bias_ref, ...), custom_call_target="tpu_custom_call" | custom-call | flops 1 | bytes 1 | tf_op jit(solution)/shard_map/head_grad/pallas_call | solution.py:288
  300.1 3.0 collective-permute-start.39
  305.7 9.1 %all-to-all-start.2 = ((bf16[32,192,128]{2,1,0:T(8,128)(2,1)}), bf16[32,192,128]{2,1,0:T(8,128)(2,1)S(1)}, u32[]{:S(2)}, u32[]{:S(2)}) async-start(bf16[32,192,128]{2,1,0:T(8,128)(2,1)} %get-tuple-element.114.grad_ref), calls=%async_computation.2 | async-start | bytes 3145728 | tf_op jit(solution)/shard_map/all_to_all | solution.py:705
  323.8 2.7 collective-permute-start.49
  327.0 13.8 %collective-permute-done.42 = bf16[416,128]{1,0:T(8,128)(2,1)S(1)} collective-permute-done((bf16[416,128]{1,0:T(8,128)(2,1)S(1)}, bf16[416,128]{1,0:T(8,128)(2,1)S(1)}, u32[]{:S(2)}, u32[]{:S(2)}) %collective-permute-start.42) | collective-permute-done | bytes 106528 | tf_op jit(solution)/shard_map/ppermute | solution.py:583
  344.3 2.7 collective-permute-start.45
  355.6 3.4 collective-permute-start.54
  360.7 13.0 %collective-permute-done.47 = bf16[4,416,128]{2,1,0:T(8,128)(2,1)S(1)} collective-permute-done((bf16[4,416,128]{2,1,0:T(8,128)(2,1)S(1)}, bf16[4,416,128]{2,1,0:T(8,128)(2,1)S(1)}, u32[]{:S(2)}, u32[]{:S(2)}) %collective-permute-start.47) | collective-permute-done | bytes 426016 | tf_op jit(solution)/shard_map/ppermute | solution.py:583
  377.4 4.5 collective-permute-start.55
  382.0 9.9 %finish.1 = (f32[128,1600]{1,0:T(8,128)}, f32[4,8,400]{2,1,0:T(8,128)S(1)}) custom-call(bf16[6144,128]{1,0:T(8,128)(2,1)S(1)} %bitcast.78, bf16[6144,1600]{1,0:T(8,128)(2,1)} %all-gather.5.cloned.1.call-done.weight_ref, bf16[128,1600]{1,0:T(8,128)(2,1)S(1)} %bitcast.81, f32[1,1600]{1,0:T(1,128)S(1)} %slice.109.gain_ref, f32[1,1600]{1,0:T(1,128)S(1)} %slice.111.shift_ref, ...), custom_call_target="tpu_custom_call" | custom-call | flops 1 | bytes 1 | tf_op jit(solution)/shard_map/finish/pallas_call | solution.py:336
  391.9 2.9 collective-permute-start.37
  399.9 6.7 %all-to-all-start.3 = ((f32[32,8,400]{2,1,0:T(8,128)}), f32[32,8,400]{2,1,0:T(8,128)S(1)}, u32[]{:S(2)}, u32[]{:S(2)}) async-start(f32[32,8,400]{2,1,0:T(8,128)} %broadcast_in_dim.29), calls=%async_computation.3 | async-start | bytes 1048576 | tf_op jit(solution)/shard_map/all_to_all | solution.py:730
  406.6 3.1 constant_dynamic-slice_fusion
  409.7 3.0 collective-permute-start.56
  414.5 3.6 all-to-all-done.3
  418.8 8.8 %unpack.1 = (f32[400,4800]{1,0:T(8,128)}, f32[400,1600]{1,0:T(8,128)}, f32[8,1600]{1,0:T(8,128)S(1)}, f32[8,1600]{1,0:T(8,128)S(1)}) custom-call(s32[3]{0:T(128)S(1)} %pad_add_fusion.1.at_ref, bf16[16,416,128]{2,1,0:T(8,128)(2,1)} %constant_dynamic-update-slice_fusion.20.left_own, bf16[16,416,128]{2,1,0:T(8,128)(2,1)} %collective-permute-done.48.left_other, ...), custom_call_target="tpu_custom_call" | custom-call | flops 1 | bytes 1 | tf_op jit(solution)/shard_map/unpack/pallas_call | solution.py:536
  427.5 4.8 %convert_element_type.103 = f32[1600,1600]{1,0:T(8,128)} convert(bf16[1600,1600]{1,0:T(8,128)(2,1)S(1)} %copy-done.21) | non-fusion elementwise | flops 2560000 | bytes 15360000 | tf_op jit(solution)/shard_map/convert_element_type | solution.py:738
  432.4 10.0 %collective-permute-done.56.refs_1_ = bf16[208,1600]{1,0:T(8,128)(2,1)S(1)} collective-permute-done((bf16[208,1600]{1,0:T(8,128)(2,1)}, bf16[208,1600]{1,0:T(8,128)(2,1)S(1)}, u32[]{:S(2)}, u32[]{:S(2)}) %collective-permute-start.56) | collective-permute-done | bytes 665632 | tf_op jit(solution)/shard_map/ppermute | solution.py:583
  443.5 3.0 collective-permute-done.60.refs_5_
  450.4 5.8 %join_columns.1 = f32[400,6400]{1,0:T(8,128)} custom-call(s32[2]{0:T(128)S(1)} %pad_add_fusion.at_ref, bf16[400,1600]{1,0:T(8,128)(2,1)S(1)} %constant_dynamic-slice_fusion.3.refs_0_, bf16[208,1600]{1,0:T(8,128)(2,1)S(1)} %collective-permute-done.56.refs_1_, bf16[208,1600]{1,0:T(8,128)(2,1)S(1)} %collective-permute-done.57.refs_2_, ...), custom_call_target="tpu_custom_call" | custom-call | flops 1 | bytes 1 | tf_op jit(solution)/shard_map/join_columns/pallas_call | solution.py:440
  (295 shorter events, 118.0 us)
Async XLA Ops:
  7.2 72.8 %all-gather.3.cloned.1.call-start = ((), (), s32[]{:S(2)}) async-start(), calls=%async_computation.5 | async-start | bytes 14057472 | tf_op jit(solution)/shard_map/all_gather | solution.py:610
  7.9 202.9 %all-gather.5.cloned.1.call-start = ((), (), s32[]{:S(2)}) async-start(), calls=%async_computation.6 | async-start | bytes 21086208 | tf_op jit(solution)/shard_map/all_gather | solution.py:654
  35.2 17.4 %collective-permute-start.3 = (bf16[208,1600]{1,0:T(8,128)(2,1)S(1)}, bf16[208,1600]{1,0:T(8,128)(2,1)}, u32[]{:S(2)}, u32[]{:S(2)}) collective-permute-start(bf16[208,1600]{1,0:T(8,128)(2,1)S(1)} %constant_dynamic-slice_fusion.13), channel_id=1, source_target_pairs={{1,0},{2,1},{3,2},{0,3},{5,4},{6,5},{7,6},{4,7},{9,8},{10,9},{11,1... | collective-permute-start | bytes 1996808 | tf_op jit(solution)/shard_map/ppermute | solution.py:583
  37.8 30.6 %collective-permute-start.5 = (bf16[208,1600]{1,0:T(8,128)(2,1)S(1)}, bf16[208,1600]{1,0:T(8,128)(2,1)}, u32[]{:S(2)}, u32[]{:S(2)}) collective-permute-start(bf16[208,1600]{1,0:T(8,128)(2,1)S(1)} %constant_dynamic-slice_fusion.13), channel_id=1, source_target_pairs={{2,0},{3,1},{0,2},{1,3},{6,4},{7,5},{4,6},{5,7},{10,8},{11,9},{8,1... | collective-permute-start | bytes 1996808 | tf_op jit(solution)/shard_map/ppermute | solution.py:583
  39.0 32.7 %collective-permute-start.7 = (bf16[208,1600]{1,0:T(8,128)(2,1)S(1)}, bf16[208,1600]{1,0:T(8,128)(2,1)}, u32[]{:S(2)}, u32[]{:S(2)}) collective-permute-start(bf16[208,1600]{1,0:T(8,128)(2,1)S(1)} %constant_dynamic-slice_fusion.13), channel_id=1, source_target_pairs={{3,0},{0,1},{1,2},{2,3},{7,4},{4,5},{5,6},{6,7},{11,8},{8,9},{9,10... | collective-permute-start | bytes 1996808 | tf_op jit(solution)/shard_map/ppermute | solution.py:583
  52.6 21.7 %collective-permute-start.4 = (bf16[208,1600]{1,0:T(8,128)(2,1)}, bf16[208,1600]{1,0:T(8,128)(2,1)}, u32[]{:S(2)}, u32[]{:S(2)}) collective-permute-start(bf16[208,1600]{1,0:T(8,128)(2,1)} %collective-permute-done.3.refs_1_), channel_id=1, source_target_pairs={{4,0},{0,4},{5,1},{1,5},{6,2},{2,6},{7,3},{3,7},{12,8},{8,12},{13,... | collective-permute-start | bytes 1996808 | tf_op jit(solution)/shard_map/ppermute | solution.py:583
  72.7 39.7 %collective-permute-start.12 = (bf16[208,1600]{1,0:T(8,128)(2,1)}, bf16[208,1600]{1,0:T(8,128)(2,1)}, u32[]{:S(2)}, u32[]{:S(2)}) collective-permute-start(bf16[208,1600]{1,0:T(8,128)(2,1)} %copy-done.17), channel_id=1, source_target_pairs={{1,0},{2,1},{3,2},{0,3},{5,4},{6,5},{7,6},{4,7},{9,8},{10,9},{11,1... | collective-permute-start | bytes 1996808 | tf_op jit(solution)/shard_map/ppermute | solution.py:583
  73.1 40.2 %collective-permute-start.13 = (bf16[208,1600]{1,0:T(8,128)(2,1)}, bf16[208,1600]{1,0:T(8,128)(2,1)}, u32[]{:S(2)}, u32[]{:S(2)}) collective-permute-start(bf16[208,1600]{1,0:T(8,128)(2,1)} %copy-done.16), channel_id=1, source_target_pairs={{2,0},{3,1},{0,2},{1,3},{6,4},{7,5},{4,6},{5,7},{10,8},{11,9},{8,1... | collective-permute-start | bytes 1996808 | tf_op jit(solution)/shard_map/ppermute | solution.py:583
  74.3 39.0 %collective-permute-start.14 = (bf16[208,1600]{1,0:T(8,128)(2,1)}, bf16[208,1600]{1,0:T(8,128)(2,1)}, u32[]{:S(2)}, u32[]{:S(2)}) collective-permute-start(bf16[208,1600]{1,0:T(8,128)(2,1)} %copy-done.15), channel_id=1, source_target_pairs={{3,0},{0,1},{1,2},{2,3},{7,4},{4,5},{5,6},{6,7},{11,8},{8,9},{9,10... | collective-permute-start | bytes 1996808 | tf_op jit(solution)/shard_map/ppermute | solution.py:583
  109.2 16.6 %collective-permute-start.15 = (bf16[128,1600]{1,0:T(8,128)(2,1)}, bf16[128,1600]{1,0:T(8,128)(2,1)}, u32[]{:S(2)}, u32[]{:S(2)}) collective-permute-start(bf16[128,1600]{1,0:T(8,128)(2,1)} %bitcast.15), channel_id=1, source_target_pairs={{1,0},{2,1},{3,2},{0,3},{5,4},{6,5},{7,6},{4,7},{9,8},{10,9},{11,1... | collective-permute-start | bytes 1228808 | tf_op jit(solution)/shard_map/ppermute | solution.py:583
  111.6 21.1 %collective-permute-start.16 = (bf16[128,1600]{1,0:T(8,128)(2,1)}, bf16[128,1600]{1,0:T(8,128)(2,1)}, u32[]{:S(2)}, u32[]{:S(2)}) collective-permute-start(bf16[128,1600]{1,0:T(8,128)(2,1)} %bitcast.15), channel_id=1, source_target_pairs={{2,0},{3,1},{0,2},{1,3},{6,4},{7,5},{4,6},{5,7},{10,8},{11,9},{8,1... | collective-permute-start | bytes 1228808 | tf_op jit(solution)/shard_map/ppermute | solution.py:583
  112.5 22.1 %collective-permute-start.17 = (bf16[128,1600]{1,0:T(8,128)(2,1)}, bf16[128,1600]{1,0:T(8,128)(2,1)}, u32[]{:S(2)}, u32[]{:S(2)}) collective-permute-start(bf16[128,1600]{1,0:T(8,128)(2,1)} %bitcast.15), channel_id=1, source_target_pairs={{3,0},{0,1},{1,2},{2,3},{7,4},{4,5},{5,6},{6,7},{11,8},{8,9},{9,10... | collective-permute-start | bytes 1228808 | tf_op jit(solution)/shard_map/ppermute | solution.py:583
  113.3 26.1 %all-to-all-start = ((bf16[32,64,128]{2,1,0:T(8,128)(2,1)}), bf16[32,64,128]{2,1,0:T(8,128)(2,1)}, u32[]{:S(2)}, u32[]{:S(2)}) async-start(bf16[32,64,128]{2,1,0:T(8,128)(2,1)} %get-tuple-element.82), calls=%async_computation | async-start | bytes 1048576 | tf_op jit(solution)/shard_map/all_to_all | solution.py:647
  123.3 283.2 %all-reduce.5.cloned.1.call-start = ((), (), s32[]{:S(2)}) async-start(), calls=%async_computation.7 | async-start | bytes 21299200 | tf_op jit(solution)/shard_map/psum | solution.py:676
  123.4 17.0 %collective-permute-start.18 = (bf16[208,1600]{1,0:T(8,128)(2,1)}, bf16[208,1600]{1,0:T(8,128)(2,1)S(1)}, u32[]{:S(2)}, u32[]{:S(2)}) collective-permute-start(bf16[208,1600]{1,0:T(8,128)(2,1)} %collective-permute-done.12.refs_1_), channel_id=1, source_target_pairs={{4,0},{0,4},{5,1},{1,5},{6,2},{2,6},{7,3},{3,7},{12,8},{8,12},{13,... | collective-permute-start | bytes 1996808 | tf_op jit(solution)/shard_map/ppermute | solution.py:583
  123.8 16.7 %collective-permute-start.19 = (bf16[208,1600]{1,0:T(8,128)(2,1)}, bf16[208,1600]{1,0:T(8,128)(2,1)S(1)}, u32[]{:S(2)}, u32[]{:S(2)}) collective-permute-start(bf16[208,1600]{1,0:T(8,128)(2,1)} %collective-permute-done.13.refs_3_), channel_id=1, source_target_pairs={{4,0},{0,4},{5,1},{1,5},{6,2},{2,6},{7,3},{3,7},{12,8},{8,12},{13,... | collective-permute-start | bytes 1996808 | tf_op jit(solution)/shard_map/ppermute | solution.py:583
  125.8 14.7 %collective-permute-start.20 = (bf16[208,1600]{1,0:T(8,128)(2,1)}, bf16[208,1600]{1,0:T(8,128)(2,1)}, u32[]{:S(2)}, u32[]{:S(2)}) collective-permute-start(bf16[208,1600]{1,0:T(8,128)(2,1)} %collective-permute-done.14.refs_5_), channel_id=1, source_target_pairs={{4,0},{0,4},{5,1},{1,5},{6,2},{2,6},{7,3},{3,7},{12,8},{8,12},{13,... | collective-permute-start | bytes 1996808 | tf_op jit(solution)/shard_map/ppermute | solution.py:583
  148.3 21.1 %collective-permute-start.23 = (bf16[128,1600]{1,0:T(8,128)(2,1)S(1)}, bf16[128,1600]{1,0:T(8,128)(2,1)S(1)}, u32[]{:S(2)}, u32[]{:S(2)}) collective-permute-start(bf16[128,1600]{1,0:T(8,128)(2,1)S(1)} %add_convert_fusion.1), channel_id=1, source_target_pairs={{3,0},{0,1},{1,2},{2,3},{7,4},{4,5},{5,6},{6,7},{11,8},{8,9},{9,10... | collective-permute-start | bytes 1228808 | tf_op jit(solution)/shard_map/ppermute | solution.py:583
  181.4 21.2 %collective-permute-start.24 = (bf16[128,1600]{1,0:T(8,128)(2,1)S(1)}, bf16[128,1600]{1,0:T(8,128)(2,1)S(1)}, u32[]{:S(2)}, u32[]{:S(2)}) collective-permute-start(bf16[128,1600]{1,0:T(8,128)(2,1)S(1)} %get-tuple-element.95), channel_id=1, source_target_pairs={{3,0},{0,1},{1,2},{2,3},{7,4},{4,5},{5,6},{6,7},{11,8},{8,9},{9,10... | collective-permute-start | bytes 1228808 | tf_op jit(solution)/shard_map/ppermute | solution.py:583
  181.4 29.4 %collective-permute-start.25 = (bf16[128,1600]{1,0:T(8,128)(2,1)}, bf16[128,1600]{1,0:T(8,128)(2,1)}, u32[]{:S(2)}, u32[]{:S(2)}) collective-permute-start(bf16[128,1600]{1,0:T(8,128)(2,1)} %get-tuple-element.96), channel_id=1, source_target_pairs={{2,0},{3,1},{0,2},{1,3},{6,4},{7,5},{4,6},{5,7},{10,8},{11,9},{8,1... | collective-permute-start | bytes 1228808 | tf_op jit(solution)/shard_map/ppermute | solution.py:583
  182.6 28.1 %collective-permute-start.26 = (bf16[128,1600]{1,0:T(8,128)(2,1)}, bf16[128,1600]{1,0:T(8,128)(2,1)}, u32[]{:S(2)}, u32[]{:S(2)}) collective-permute-start(bf16[128,1600]{1,0:T(8,128)(2,1)} %get-tuple-element.97), channel_id=1, source_target_pairs={{1,0},{2,1},{3,2},{0,3},{5,4},{6,5},{7,6},{4,7},{9,8},{10,9},{11,1... | collective-permute-start | bytes 1228808 | tf_op jit(solution)/shard_map/ppermute | solution.py:583
  220.0 24.0 %collective-permute-start.27 = (bf16[128,1600]{1,0:T(8,128)(2,1)}, bf16[128,1600]{1,0:T(8,128)(2,1)}, u32[]{:S(2)}, u32[]{:S(2)}) collective-permute-start(bf16[128,1600]{1,0:T(8,128)(2,1)} %get-tuple-element.105), channel_id=1, source_target_pairs={{1,0},{2,1},{3,2},{0,3},{5,4},{6,5},{7,6},{4,7},{9,8},{10,9},{11,1... | collective-permute-start | bytes 1228808 | tf_op jit(solution)/shard_map/ppermute | solution.py:583
  220.1 24.9 %collective-permute-start.28 = (bf16[128,1600]{1,0:T(8,128)(2,1)}, bf16[128,1600]{1,0:T(8,128)(2,1)S(1)}, u32[]{:S(2)}, u32[]{:S(2)}) collective-permute-start(bf16[128,1600]{1,0:T(8,128)(2,1)} %get-tuple-element.105), channel_id=1, source_target_pairs={{2,0},{3,1},{0,2},{1,3},{6,4},{7,5},{4,6},{5,7},{10,8},{11,9},{8,1... | collective-permute-start | bytes 1228808 | tf_op jit(solution)/shard_map/ppermute | solution.py:583
  220.9 16.5 %collective-permute-start.35 = (bf16[400,128]{1,0:T(8,128)(2,1)}, bf16[400,128]{1,0:T(8,128)(2,1)S(1)}, u32[]{:S(2)}, u32[]{:S(2)}) collective-permute-start(bf16[400,128]{1,0:T(8,128)(2,1)} %get-tuple-element.167), channel_id=1, source_target_pairs={{3,0},{0,1},{1,2},{2,3},{7,4},{4,5},{5,6},{6,7},{11,8},{8,9},{9,10... | collective-permute-start | bytes 307208 | tf_op jit(solution)/shard_map/ppermute | solution.py:583
  222.2 16.9 %collective-permute-start.34 = (bf16[400,128]{1,0:T(8,128)(2,1)S(1)}, bf16[400,128]{1,0:T(8,128)(2,1)S(1)}, u32[]{:S(2)}, u32[]{:S(2)}) collective-permute-start(bf16[400,128]{1,0:T(8,128)(2,1)S(1)} %get-tuple-element.168), channel_id=1, source_target_pairs={{2,0},{3,1},{0,2},{1,3},{6,4},{7,5},{4,6},{5,7},{10,8},{11,9},{8,1... | collective-permute-start | bytes 307208 | tf_op jit(solution)/shard_map/ppermute | solution.py:583
  225.9 18.0 %collective-permute-start.33 = (bf16[400,128]{1,0:T(8,128)(2,1)S(1)}, bf16[400,128]{1,0:T(8,128)(2,1)S(1)}, u32[]{:S(2)}, u32[]{:S(2)}) collective-permute-start(bf16[400,128]{1,0:T(8,128)(2,1)S(1)} %get-tuple-element.169), channel_id=1, source_target_pairs={{1,0},{2,1},{3,2},{0,3},{5,4},{6,5},{7,6},{4,7},{9,8},{10,9},{11,1... | collective-permute-start | bytes 307208 | tf_op jit(solution)/shard_map/ppermute | solution.py:583
  227.9 24.4 %all-to-all-start.1 = ((bf16[32,64,128]{2,1,0:T(8,128)(2,1)}), bf16[32,64,128]{2,1,0:T(8,128)(2,1)S(1)}, u32[]{:S(2)}, u32[]{:S(2)}) async-start(bf16[32,64,128]{2,1,0:T(8,128)(2,1)} %bitcast.17), calls=%async_computation.1 | async-start | bytes 1048576 | tf_op jit(solution)/shard_map/all_to_all | solution.py:683
  252.3 53.4 %all-to-all-start.4 = ((bf16[32,16,1600]{2,1,0:T(8,128)(2,1)}), bf16[32,16,1600]{2,1,0:T(8,128)(2,1)S(1)}, u32[]{:S(2)}, u32[]{:S(2)}) async-start(bf16[32,16,1600]{2,1,0:T(8,128)(2,1)} %out_grad.1), calls=%async_computation.4 | async-start | bytes 3407872 | tf_op jit(solution)/shard_map/all_to_all | solution.py:702
  260.4 25.2 %collective-permute-start.32 = (bf16[128,1600]{1,0:T(8,128)(2,1)}, bf16[128,1600]{1,0:T(8,128)(2,1)S(1)}, u32[]{:S(2)}, u32[]{:S(2)}) collective-permute-start(bf16[128,1600]{1,0:T(8,128)(2,1)} %get-tuple-element.108), channel_id=1, source_target_pairs={{1,0},{2,1},{3,2},{0,3},{5,4},{6,5},{7,6},{4,7},{9,8},{10,9},{11,1... | collective-permute-start | bytes 1228808 | tf_op jit(solution)/shard_map/ppermute | solution.py:583
  260.5 25.1 %collective-permute-start.31 = (bf16[128,1600]{1,0:T(8,128)(2,1)}, bf16[128,1600]{1,0:T(8,128)(2,1)S(1)}, u32[]{:S(2)}, u32[]{:S(2)}) collective-permute-start(bf16[128,1600]{1,0:T(8,128)(2,1)} %get-tuple-element.107), channel_id=1, source_target_pairs={{2,0},{3,1},{0,2},{1,3},{6,4},{7,5},{4,6},{5,7},{10,8},{11,9},{8,1... | collective-permute-start | bytes 1228808 | tf_op jit(solution)/shard_map/ppermute | solution.py:583
  262.7 22.9 %collective-permute-start.30 = (bf16[128,1600]{1,0:T(8,128)(2,1)}, bf16[128,1600]{1,0:T(8,128)(2,1)S(1)}, u32[]{:S(2)}, u32[]{:S(2)}) collective-permute-start(bf16[128,1600]{1,0:T(8,128)(2,1)} %get-tuple-element.106), channel_id=1, source_target_pairs={{3,0},{0,1},{1,2},{2,3},{7,4},{4,5},{5,6},{6,7},{11,8},{8,9},{9,10... | collective-permute-start | bytes 1228808 | tf_op jit(solution)/shard_map/ppermute | solution.py:583
  300.1 14.7 %collective-permute-start.39 = (bf16[416,192]{1,0:T(8,128)(2,1)}, bf16[416,192]{1,0:T(8,128)(2,1)S(1)}, u32[]{:S(2)}, u32[]{:S(2)}) collective-permute-start(bf16[416,192]{1,0:T(8,128)(2,1)} %get-tuple-element.121), channel_id=1, source_target_pairs={{1,0},{2,1},{3,2},{0,3},{5,4},{6,5},{7,6},{4,7},{9,8},{10,9},{11,1... | collective-permute-start | bytes 479240 | tf_op jit(solution)/shard_map/ppermute | solution.py:583
  305.7 76.3 %all-to-all-start.2 = ((bf16[32,192,128]{2,1,0:T(8,128)(2,1)}), bf16[32,192,128]{2,1,0:T(8,128)(2,1)S(1)}, u32[]{:S(2)}, u32[]{:S(2)}) async-start(bf16[32,192,128]{2,1,0:T(8,128)(2,1)} %get-tuple-element.114.grad_ref), calls=%async_computation.2 | async-start | bytes 3145728 | tf_op jit(solution)/shard_map/all_to_all | solution.py:705
  318.7 22.1 %collective-permute-start.42 = (bf16[416,128]{1,0:T(8,128)(2,1)S(1)}, bf16[416,128]{1,0:T(8,128)(2,1)S(1)}, u32[]{:S(2)}, u32[]{:S(2)}) collective-permute-start(bf16[416,128]{1,0:T(8,128)(2,1)S(1)} %get-tuple-element.124), channel_id=1, source_target_pairs={{8,0},{16,8},{24,16},{0,24},{9,1},{17,9},{25,17},{1,25},{10,2},{18... | collective-permute-start | bytes 319496 | tf_op jit(solution)/shard_map/ppermute | solution.py:583
  321.3 20.9 %collective-permute-start.43 = (bf16[416,128]{1,0:T(8,128)(2,1)S(1)}, bf16[416,128]{1,0:T(8,128)(2,1)S(1)}, u32[]{:S(2)}, u32[]{:S(2)}) collective-permute-start(bf16[416,128]{1,0:T(8,128)(2,1)S(1)} %get-tuple-element.124), channel_id=1, source_target_pairs={{16,0},{24,8},{0,16},{8,24},{17,1},{25,9},{1,17},{9,25},{18,2},{26... | collective-permute-start | bytes 319496 | tf_op jit(solution)/shard_map/ppermute | solution.py:583
  321.9 22.4 %collective-permute-start.44 = (bf16[416,128]{1,0:T(8,128)(2,1)S(1)}, bf16[416,128]{1,0:T(8,128)(2,1)S(1)}, u32[]{:S(2)}, u32[]{:S(2)}) collective-permute-start(bf16[416,128]{1,0:T(8,128)(2,1)S(1)} %get-tuple-element.124), channel_id=1, source_target_pairs={{24,0},{0,8},{8,16},{16,24},{25,1},{1,9},{9,17},{17,25},{26,2},{2,... | collective-permute-start | bytes 319496 | tf_op jit(solution)/shard_map/ppermute | solution.py:583
  323.8 23.9 %collective-permute-start.49 = (bf16[416,128]{1,0:T(8,128)(2,1)S(1)}, bf16[416,128]{1,0:T(8,128)(2,1)S(1)}, u32[]{:S(2)}, u32[]{:S(2)}) collective-permute-start(bf16[416,128]{1,0:T(8,128)(2,1)S(1)} %get-tuple-element.126), channel_id=1, source_target_pairs={{32,0},{64,32},{96,64},{0,96},{33,1},{65,33},{97,65},{1,97},{34,2}... | collective-permute-start | bytes 319496 | tf_op jit(solution)/shard_map/ppermute | solution.py:583
  326.5 21.8 %collective-permute-start.50 = (bf16[416,128]{1,0:T(8,128)(2,1)S(1)}, bf16[416,128]{1,0:T(8,128)(2,1)S(1)}, u32[]{:S(2)}, u32[]{:S(2)}) collective-permute-start(bf16[416,128]{1,0:T(8,128)(2,1)S(1)} %get-tuple-element.126), channel_id=1, source_target_pairs={{64,0},{96,32},{0,64},{32,96},{65,1},{97,33},{1,65},{33,97},{66,2}... | collective-permute-start | bytes 319496 | tf_op jit(solution)/shard_map/ppermute | solution.py:583
  347.7 26.1 %collective-permute-start.47 = (bf16[4,416,128]{2,1,0:T(8,128)(2,1)S(1)}, bf16[4,416,128]{2,1,0:T(8,128)(2,1)S(1)}, u32[]{:S(2)}, u32[]{:S(2)}) collective-permute-start(bf16[4,416,128]{2,1,0:T(8,128)(2,1)S(1)} %pad_maximum_fusion), channel_id=1, source_target_pairs={{96,0},{0,32},{32,64},{64,96},{97,1},{1,33},{33,65},{65,97},{98,2}... | collective-permute-start | bytes 1277960 | tf_op jit(solution)/shard_map/ppermute | solution.py:583
  348.3 26.6 %collective-permute-start.52 = (bf16[4,416,128]{2,1,0:T(8,128)(2,1)S(1)}, bf16[4,416,128]{2,1,0:T(8,128)(2,1)S(1)}, u32[]{:S(2)}, u32[]{:S(2)}) collective-permute-start(bf16[4,416,128]{2,1,0:T(8,128)(2,1)S(1)} %pad_maximum_fusion.1), channel_id=1, source_target_pairs={{8,0},{16,8},{24,16},{0,24},{9,1},{17,9},{25,17},{1,25},{10,2},{18... | collective-permute-start | bytes 1277960 | tf_op jit(solution)/shard_map/ppermute | solution.py:583
  350.4 25.4 %collective-permute-start.53 = (bf16[4,416,128]{2,1,0:T(8,128)(2,1)S(1)}, bf16[4,416,128]{2,1,0:T(8,128)(2,1)S(1)}, u32[]{:S(2)}, u32[]{:S(2)}) collective-permute-start(bf16[4,416,128]{2,1,0:T(8,128)(2,1)S(1)} %pad_maximum_fusion.1), channel_id=1, source_target_pairs={{16,0},{24,8},{0,16},{8,24},{17,1},{25,9},{1,17},{9,25},{18,2},{26... | collective-permute-start | bytes 1277960 | tf_op jit(solution)/shard_map/ppermute | solution.py:583
  355.6 21.0 %collective-permute-start.54 = (bf16[4,416,128]{2,1,0:T(8,128)(2,1)S(1)}, bf16[4,416,128]{2,1,0:T(8,128)(2,1)S(1)}, u32[]{:S(2)}, u32[]{:S(2)}) collective-permute-start(bf16[4,416,128]{2,1,0:T(8,128)(2,1)S(1)} %pad_maximum_fusion.1), channel_id=1, source_target_pairs={{24,0},{0,8},{8,16},{16,24},{25,1},{1,9},{9,17},{17,25},{26,2},{2,... | collective-permute-start | bytes 1277960 | tf_op jit(solution)/shard_map/ppermute | solution.py:583
  374.5 44.3 %collective-permute-start.48 = (bf16[16,416,128]{2,1,0:T(8,128)(2,1)}, bf16[16,416,128]{2,1,0:T(8,128)(2,1)}, u32[]{:S(2)}, u32[]{:S(2)}) collective-permute-start(bf16[16,416,128]{2,1,0:T(8,128)(2,1)} %constant_dynamic-update-slice_fusion.20.left_own), channel_id=1, source_target_pairs={{4,0},{0,4},{5,1},{1,5},{6,2},{2,6},{7,3},{3,7},{12,8},{8,12},{13,... | collective-permute-start | bytes 5111816 | tf_op jit(solution)/shard_map/ppermute | solution.py:583
  377.4 41.4 %collective-permute-start.55 = (bf16[16,416,128]{2,1,0:T(8,128)(2,1)}, bf16[16,416,128]{2,1,0:T(8,128)(2,1)}, u32[]{:S(2)}, u32[]{:S(2)}) collective-permute-start(bf16[16,416,128]{2,1,0:T(8,128)(2,1)} %constant_dynamic-update-slice_fusion.27.right_own), channel_id=1, source_target_pairs={{4,0},{0,4},{5,1},{1,5},{6,2},{2,6},{7,3},{3,7},{12,8},{8,12},{13,... | collective-permute-start | bytes 5111816 | tf_op jit(solution)/shard_map/ppermute | solution.py:583
  399.9 18.2 %all-to-all-start.3 = ((f32[32,8,400]{2,1,0:T(8,128)}), f32[32,8,400]{2,1,0:T(8,128)S(1)}, u32[]{:S(2)}, u32[]{:S(2)}) async-start(f32[32,8,400]{2,1,0:T(8,128)} %broadcast_in_dim.29), calls=%async_computation.3 | async-start | bytes 1048576 | tf_op jit(solution)/shard_map/all_to_all | solution.py:730
  409.7 32.6 %collective-permute-start.56 = (bf16[208,1600]{1,0:T(8,128)(2,1)}, bf16[208,1600]{1,0:T(8,128)(2,1)S(1)}, u32[]{:S(2)}, u32[]{:S(2)}) collective-permute-start(bf16[208,1600]{1,0:T(8,128)(2,1)} %get-tuple-element.154), channel_id=1, source_target_pairs={{1,0},{2,1},{3,2},{0,3},{5,4},{6,5},{7,6},{4,7},{9,8},{10,9},{11,1... | collective-permute-start | bytes 1996808 | tf_op jit(solution)/shard_map/ppermute | solution.py:583
  412.6 30.9 %collective-permute-start.58 = (bf16[208,1600]{1,0:T(8,128)(2,1)}, bf16[208,1600]{1,0:T(8,128)(2,1)S(1)}, u32[]{:S(2)}, u32[]{:S(2)}) collective-permute-start(bf16[208,1600]{1,0:T(8,128)(2,1)} %get-tuple-element.153), channel_id=1, source_target_pairs={{2,0},{3,1},{0,2},{1,3},{6,4},{7,5},{4,6},{5,7},{10,8},{11,9},{8,1... | collective-permute-start | bytes 1996808 | tf_op jit(solution)/shard_map/ppermute | solution.py:583
  412.6 33.9 %collective-permute-start.60 = (bf16[208,1600]{1,0:T(8,128)(2,1)}, bf16[208,1600]{1,0:T(8,128)(2,1)S(1)}, u32[]{:S(2)}, u32[]{:S(2)}) collective-permute-start(bf16[208,1600]{1,0:T(8,128)(2,1)} %get-tuple-element.152), channel_id=1, source_target_pairs={{3,0},{0,1},{1,2},{2,3},{7,4},{4,5},{5,6},{6,7},{11,8},{8,9},{9,10... | collective-permute-start | bytes 1996808 | tf_op jit(solution)/shard_map/ppermute | solution.py:583
  (60 other events, 441.6 us)
Sparse Core Ops, SparseCore 0:
  10.3 68.9 all-gather.2
  81.5 86.2 all-gather.4
  227.2 172.4 all-reduce.4
where the time goes:
time: 472 us; the launch traced here: 463 us
  starting transfers between devices  136 us (29%)
  waiting for transfers between devices  109 us (23%)
  Pallas kernels  90.3 us (19%)
  local copies, waits for them, and re-layouts  57 us (12%)
  matrix products  40.7 us (9%)
  between operations  15.1 us (3%)
  other arithmetic  15 us (3%)
    ppermute x62, waiting for transfers between devices, shift(): return lax.ppermute(array, axis, [((i + k) % size, i) for i in range(size)])  101 us
    ppermute x62, starting transfers between devices, shift(): return lax.ppermute(array, axis, [((i + k) % size, i) for i in range(size)])  92.7 us
    dot_general x8, matrix products, mm(): return lax.dot_general(left, right, dims, preferred_element_type=F32)  40.7 us
    unnamed x110, local copies, waits for them, and re-layouts  36.1 us
    pallas_call x1, Pallas kernels, attend(): pl.pallas_call(functools.partial(attend_kernel, seqs, rows, half), grid=(...  26.9 us
    pallas_call x1, Pallas kernels, attend_back(): pl.pallas_call(functools.partial(attend_back_kernel, seqs, rows, half), i...  21.2 us
    all_to_all x1, starting transfers between devices, on_device(): lax.all_to_all(mixed_turned, CTX, 0, 0).reshape(n_ctx * HD, tokens)[:width]  10 us
    pallas_call x1, Pallas kernels, finish(): pl.pallas_call(functools.partial(finish_kernel, n_w), grid=(5,), in_specs...  9.89 us
  transfers between devices with their start and end apart: 70, of which 21 were waited for; matrix products, arithmetic and copies ran while one was open for 18% of the time, Pallas kernels for 18%

commit v1 on v0

--- a/solution.py
+++ b/solution.py
@@ -299,7 +299,7 @@
             jax.ShapeDtypeStruct((rows, 3 * HD), BF if k else F32) for k in range(n_w)
         ],
         scratch_shapes=[pltpu.VMEM((3 * HD, width), F32), pltpu.VMEM((width, 3 * HD), F32)],
-        compiler_params=pltpu.CompilerParams(vmem_limit_bytes=32 << 20),
+        compiler_params=pltpu.CompilerParams(vmem_limit_bytes=56 << 20),
         cost_estimate=pl.CostEstimate(flops=1, bytes_accessed=1, transcendentals=0),
         name="head_grad",
     )(at, grads, bias, gathered)

time: 472 us -> 466 us (0.987)
  local copies, waits for them, and re-layouts: 57 us -> 50.6 us
    unnamed x110 -> x98, local copies, waits for them, and re-layouts: 36.1 us -> 30.4 us
  transfers between devices with their start and end apart: 70 -> 70, of which waited for: 21 -> 21; matrix products, arithmetic and copies ran while one was open for 18% -> 18% of each run, Pallas kernels for 18% -> 19%
where the time goes in v1:
time: 466 us; the launch traced here: 458 us
  starting transfers between devices  136 us (29%)
  waiting for transfers between devices  106 us (23%)
  Pallas kernels  93.5 us (20%)
  local copies, waits for them, and re-layouts  50.6 us (11%)
  matrix products  40.7 us (9%)
  other arithmetic  16.3 us (3%)
  between operations  15.1 us (3%)
    ppermute x62, waiting for transfers between devices, shift(): return lax.ppermute(array, axis, [((i + k) % size, i) for i in range(size)])  99.9 us
    ppermute x62, starting transfers between devices, shift(): return lax.ppermute(array, axis, [((i + k) % size, i) for i in range(size)])  91.6 us
    dot_general x8, matrix products, mm(): return lax.dot_general(left, right, dims, preferred_element_type=F32)  40.7 us
    unnamed x98, local copies, waits for them, and re-layouts  30.4 us
    pallas_call x1, Pallas kernels, attend(): pl.pallas_call(functools.partial(attend_kernel, seqs, rows, half), grid=(...  26.9 us
    pallas_call x1, Pallas kernels, attend_back(): pl.pallas_call(functools.partial(attend_back_kernel, seqs, rows, half), i...  21.3 us
    pallas_call x1, Pallas kernels, head_grad(): pl.pallas_call(functools.partial(head_grad_kernel, n_w), grid=(n_ctx // g...  11.1 us
    all_to_all x1, starting transfers between devices, on_device(): lax.all_to_all(mixed_turned, CTX, 0, 0).reshape(n_ctx * HD, tokens)[:width]  10 us
  transfers between devices with their start and end apart: 70, of which 21 were waited for; matrix products, arithmetic and copies ran while one was open for 18% of the time, Pallas kernels for 19%

profile of v1, /device:TPU:1, one launch (start us, length us, event | category | flops | bytes accessed | tf_op | source)
XLA Modules:
  0.0 458.0 jit_solution(5788602763166629032)
XLA Ops:
  9.3 3.4 collective-permute-start
  13.8 3.8 collective-permute-done
  19.8 5.7 %collective-permute-done.2 = bf16[400,192]{1,0:T(8,128)(2,1)S(1)} collective-permute-done((bf16[400,192]{1,0:T(8,128)(2,1)S(1)}, bf16[400,192]{1,0:T(8,128)(2,1)S(1)}, u32[]{:S(2)}, u32[]{:S(2)}) %collective-permute-start.2) | collective-permute-done | bytes 153632 | tf_op jit(solution)/shard_map/ppermute | solution.py:583
  28.6 2.5 copy-done.1
  35.2 2.6 collective-permute-start.3
  39.8 12.8 %collective-permute-done.3.refs_1_ = bf16[208,1600]{1,0:T(8,128)(2,1)} collective-permute-done((bf16[208,1600]{1,0:T(8,128)(2,1)S(1)}, bf16[208,1600]{1,0:T(8,128)(2,1)}, u32[]{:S(2)}, u32[]{:S(2)}) %collective-permute-start.3) | collective-permute-done | bytes 665632 | tf_op jit(solution)/shard_map/ppermute | solution.py:583
  52.6 15.8 %collective-permute-start.4 = (bf16[208,1600]{1,0:T(8,128)(2,1)}, bf16[208,1600]{1,0:T(8,128)(2,1)}, u32[]{:S(2)}, u32[]{:S(2)}) collective-permute-start(bf16[208,1600]{1,0:T(8,128)(2,1)} %collective-permute-done.3.refs_1_), channel_id=1, source_target_pairs={{4,0},{0,4},{5,1},{1,5},{6,2},{2,6},{7,3},{3,7},{12,8},{8,12},{13,... | collective-permute-start | bytes 1996808 | tf_op jit(solution)/shard_map/ppermute | solution.py:583
  68.4 3.3 collective-permute-done.7.refs_5_
  75.0 2.6 join_rows.2
  80.0 26.9 %attend.1 = (bf16[4096,1600]{1,0:T(8,128)(2,1)}, bf16[4096,192]{1,0:T(8,128)(2,1)S(1)}, bf16[32,64,128]{2,1,0:T(8,128)(2,1)}, f32[2,64,2048]{2,1,0:T(8,128)S(1)}, f32[2,1,2048]{2,1,0:T(1,128)S(1)}) custom-call(s32[2,64]{1,0:T(2,128)S(1)} %copy-done.15, bf16[4096,1600]{1,0:T(8,128)(2,1)} %all-gather.3.cloned.1.call-done.in_ref, ...), custom_call_target="tpu_custom_call" | custom-call | flops 20000000000 | bytes 20000000 | tf_op jit(solution)/shard_map/attend/pallas_call | solution.py:132
  113.3 10.0 %all-to-all-start = ((bf16[32,64,128]{2,1,0:T(8,128)(2,1)}), bf16[32,64,128]{2,1,0:T(8,128)(2,1)}, u32[]{:S(2)}, u32[]{:S(2)}) async-start(bf16[32,64,128]{2,1,0:T(8,128)(2,1)} %get-tuple-element.82), calls=%async_computation | async-start | bytes 1048576 | tf_op jit(solution)/shard_map/all_to_all | solution.py:647
  125.8 5.1 %collective-permute-start.20 = (bf16[208,1600]{1,0:T(8,128)(2,1)}, bf16[208,1600]{1,0:T(8,128)(2,1)}, u32[]{:S(2)}, u32[]{:S(2)}) collective-permute-start(bf16[208,1600]{1,0:T(8,128)(2,1)} %collective-permute-done.14.refs_5_), channel_id=1, source_target_pairs={{4,0},{0,4},{5,1},{1,5},{6,2},{2,6},{7,3},{3,7},{12,8},{8,12},{13,... | collective-permute-start | bytes 1996808 | tf_op jit(solution)/shard_map/ppermute | solution.py:583
  136.4 3.0 all-to-all-done
  140.4 4.1 fusion.8
  148.5 5.9 %fusion.11 = f32[512,1600]{0,1:T(8,128)S(1)} fusion(bf16[512,1600]{1,0:T(8,128)(2,1)} %constant_dynamic-update-slice_fusion.8, bf16[1600,1600]{1,0:T(8,128)(2,1)} %param.23), kind=kOutput, calls=%fused_computation.115 | convolution fusion | flops 2621440000 | bytes 10035200 | tf_op jit(solution)/shard_map/dot_general | solution.py:24
  157.6 11.9 %collective-permute-done.23 = bf16[128,1600]{1,0:T(8,128)(2,1)S(1)} collective-permute-done((bf16[128,1600]{1,0:T(8,128)(2,1)S(1)}, bf16[128,1600]{1,0:T(8,128)(2,1)S(1)}, u32[]{:S(2)}, u32[]{:S(2)}) %collective-permute-start.23) | collective-permute-done | bytes 409632 | tf_op jit(solution)/shard_map/ppermute | solution.py:583
  169.7 3.2 convolution_add_fusion
  175.2 5.3 %fusion.9 = (bf16[512,1600]{1,0:T(8,128)(2,1)S(1)}, f32[512,1600]{1,0:T(8,128)}) fusion(bf16[512,1600]{0,1:T(8,128)(2,1)S(1)} %get-tuple-element.100, bf16[1600,1600]{1,0:T(8,128)(2,1)S(1)} %join_rows.3), kind=kOutput, calls=%fused_computation.113 | convolution fusion | flops 2622259200 | bytes 11673600 | tf_op jit(solution)/shard_map/dot_general | solution.py:24
  185.7 5.7 %convolution_convert_fusion = bf16[1600,1600]{1,0:T(8,128)(2,1)} fusion(bf16[512,1600]{1,0:T(8,128)(2,1)S(1)} %constant_dynamic-update-slice_fusion.12, bf16[512,1600]{0,1:T(8,128)(2,1)S(1)} %get-tuple-element.100), kind=kOutput, calls=%fused_computation | convolution fusion | flops 2624000000 | bytes 8396800 | tf_op jit(solution)/shard_map/dot_general | solution.py:24
  191.3 6.3 %convolution_convert_fusion.1 = bf16[1600,1600]{1,0:T(8,128)(2,1)} fusion(bf16[512,1600]{0,1:T(8,128)(2,1)S(1)} %get-tuple-element.99, bf16[512,1600]{1,0:T(8,128)(2,1)} %constant_dynamic-update-slice_fusion.8), kind=kOutput, calls=%fused_computation.1 | convolution fusion | flops 2624000000 | bytes 8396800 | tf_op jit(solution)/shard_map/dot_general | solution.py:24
  197.6 5.2 %collective-permute-done.24 = bf16[128,1600]{1,0:T(8,128)(2,1)S(1)} collective-permute-done((bf16[128,1600]{1,0:T(8,128)(2,1)S(1)}, bf16[128,1600]{1,0:T(8,128)(2,1)S(1)}, u32[]{:S(2)}, u32[]{:S(2)}) %collective-permute-start.24) | collective-permute-done | bytes 409632 | tf_op jit(solution)/shard_map/ppermute | solution.py:583
  202.8 6.1 %fusion.10 = (bf16[512,1600]{1,0:T(8,128)(2,1)S(1)}, f32[512,1600]{1,0:T(8,128)S(1)}) fusion(bf16[512,1600]{0,1:T(8,128)(2,1)S(1)} %get-tuple-element.99, bf16[1600,1600]{1,0:T(8,128)(2,1)} %param.23), kind=kOutput, calls=%fused_computation.114 | convolution fusion | flops 2622259200 | bytes 11673600 | tf_op jit(solution)/shard_map/dot_general | solution.py:24
  213.5 2.5 convert_reduce_fusion.1
  216.0 4.2 convolution_convert_fusion.2
  222.4 3.7 collective-permute-start.34
  228.2 9.1 %all-to-all-start.1 = ((bf16[32,64,128]{2,1,0:T(8,128)(2,1)}), bf16[32,64,128]{2,1,0:T(8,128)(2,1)S(1)}, u32[]{:S(2)}, u32[]{:S(2)}) async-start(bf16[32,64,128]{2,1,0:T(8,128)(2,1)} %bitcast.17), calls=%async_computation.1 | async-start | bytes 1048576 | tf_op jit(solution)/shard_map/all_to_all | solution.py:683
  239.0 5.1 %collective-permute-done.33 = bf16[400,128]{1,0:T(8,128)(2,1)S(1)} collective-permute-done((bf16[400,128]{1,0:T(8,128)(2,1)S(1)}, bf16[400,128]{1,0:T(8,128)(2,1)S(1)}, u32[]{:S(2)}, u32[]{:S(2)}) %collective-permute-start.33) | collective-permute-done | bytes 102432 | tf_op jit(solution)/shard_map/ppermute | solution.py:583
  245.3 4.8 %collective-permute-done.29 = bf16[128,1600]{1,0:T(8,128)(2,1)S(1)} collective-permute-done((bf16[128,1600]{1,0:T(8,128)(2,1)}, bf16[128,1600]{1,0:T(8,128)(2,1)S(1)}, u32[]{:S(2)}, u32[]{:S(2)}) %collective-permute-start.29) | collective-permute-done | bytes 409632 | tf_op jit(solution)/shard_map/ppermute | solution.py:583
  252.2 8.1 %all-to-all-start.4 = ((bf16[32,16,1600]{2,1,0:T(8,128)(2,1)}), bf16[32,16,1600]{2,1,0:T(8,128)(2,1)S(1)}, u32[]{:S(2)}, u32[]{:S(2)}) async-start(bf16[32,16,1600]{2,1,0:T(8,128)(2,1)} %out_grad.1), calls=%async_computation.4 | async-start | bytes 3407872 | tf_op jit(solution)/shard_map/all_to_all | solution.py:702
  264.3 21.3 %attend_back.1 = (bf16[32,192,128]{2,1,0:T(8,128)(2,1)}, f32[1,192]{1,0:T(1,128)S(1)}) custom-call(s32[2,64]{1,0:T(2,128)S(1)} %copy-done.15, bf16[4096,192]{1,0:T(8,128)(2,1)S(1)} %copy-done.8, f32[2,64,2048]{2,1,0:T(8,128)S(1)} %copy-done.10, f32[2,1,2048]{2,1,0:T(1,128)S(1)} %get-tuple-element.111.log_ref, bf16[32,64,128]{2,1,0:T(8,128)(2,1)S(1)} %all-to-all-done.1.grad_ref), custom_call_target="tpu_custom_call" | custom-call | flops 1 | bytes 1 | tf_op jit(solution)/shard_map/attend_back/pallas_call | solution.py:240
  286.2 11.1 %head_grad.1 = (f32[416,192]{1,0:T(8,128)}, bf16[416,192]{1,0:T(8,128)(2,1)}, bf16[416,192]{1,0:T(8,128)(2,1)}, bf16[416,192]{1,0:T(8,128)(2,1)}) custom-call(s32[2]{0:T(128)} %copy-done.12, bf16[32,192,128]{2,1,0:T(8,128)(2,1)} %get-tuple-element.114.grad_ref, f32[1,192]{1,0:T(1,128)} %copy-done.14, bf16[4096,1600]{1,0:T(8,128)(2,1)} %get-tuple-element.119.in_ref), custom_call_target="tpu_custom_call" | custom-call | flops 1 | bytes 1 | tf_op jit(solution)/shard_map/head_grad/pallas_call | solution.py:288
  297.3 2.9 collective-permute-start.39
  302.3 9.1 %all-to-all-start.2 = ((bf16[32,192,128]{2,1,0:T(8,128)(2,1)}), bf16[32,192,128]{2,1,0:T(8,128)(2,1)S(1)}, u32[]{:S(2)}, u32[]{:S(2)}) async-start(bf16[32,192,128]{2,1,0:T(8,128)(2,1)} %get-tuple-element.114.grad_ref), calls=%async_computation.2 | async-start | bytes 3145728 | tf_op jit(solution)/shard_map/all_to_all | solution.py:705
  315.8 2.6 collective-permute-start.42
  324.1 11.4 %collective-permute-done.42 = bf16[416,128]{1,0:T(8,128)(2,1)S(1)} collective-permute-done((bf16[416,128]{1,0:T(8,128)(2,1)S(1)}, bf16[416,128]{1,0:T(8,128)(2,1)S(1)}, u32[]{:S(2)}, u32[]{:S(2)}) %collective-permute-start.42) | collective-permute-done | bytes 106528 | tf_op jit(solution)/shard_map/ppermute | solution.py:583
  339.0 2.6 collective-permute-start.45
  342.4 3.0 collective-permute-start.52
  354.2 13.6 %collective-permute-done.47 = bf16[4,416,128]{2,1,0:T(8,128)(2,1)S(1)} collective-permute-done((bf16[4,416,128]{2,1,0:T(8,128)(2,1)S(1)}, bf16[4,416,128]{2,1,0:T(8,128)(2,1)S(1)}, u32[]{:S(2)}, u32[]{:S(2)}) %collective-permute-start.47) | collective-permute-done | bytes 426016 | tf_op jit(solution)/shard_map/ppermute | solution.py:583
  371.5 5.4 %collective-permute-start.55 = (bf16[16,416,128]{2,1,0:T(8,128)(2,1)}, bf16[16,416,128]{2,1,0:T(8,128)(2,1)}, u32[]{:S(2)}, u32[]{:S(2)}) collective-permute-start(bf16[16,416,128]{2,1,0:T(8,128)(2,1)} %constant_dynamic-update-slice_fusion.27.right_own), channel_id=1, source_target_pairs={{4,0},{0,4},{5,1},{1,5},{6,2},{2,6},{7,3},{3,7},{12,8},{8,12},{13,... | collective-permute-start | bytes 5111816 | tf_op jit(solution)/shard_map/ppermute | solution.py:583
  376.9 10.0 %finish.1 = (f32[128,1600]{1,0:T(8,128)}, f32[4,8,400]{2,1,0:T(8,128)S(1)}) custom-call(bf16[6144,128]{1,0:T(8,128)(2,1)S(1)} %bitcast.78, bf16[6144,1600]{1,0:T(8,128)(2,1)} %all-gather.5.cloned.1.call-done.weight_ref, bf16[128,1600]{1,0:T(8,128)(2,1)S(1)} %bitcast.81, f32[1,1600]{1,0:T(1,128)S(1)} %slice.109.gain_ref, f32[1,1600]{1,0:T(1,128)S(1)} %slice.111.shift_ref, ...), custom_call_target="tpu_custom_call" | custom-call | flops 1 | bytes 1 | tf_op jit(solution)/shard_map/finish/pallas_call | solution.py:336
  393.5 8.1 %all-to-all-start.3 = ((f32[32,8,400]{2,1,0:T(8,128)}), f32[32,8,400]{2,1,0:T(8,128)S(1)}, u32[]{:S(2)}, u32[]{:S(2)}) async-start(f32[32,8,400]{2,1,0:T(8,128)} %broadcast_in_dim.29), calls=%async_computation.3 | async-start | bytes 1048576 | tf_op jit(solution)/shard_map/all_to_all | solution.py:730
  401.6 2.9 constant_dynamic-slice_fusion
  404.5 2.9 collective-permute-start.56
  413.8 8.8 %unpack.1 = (f32[400,4800]{1,0:T(8,128)}, f32[400,1600]{1,0:T(8,128)}, f32[8,1600]{1,0:T(8,128)S(1)}, f32[8,1600]{1,0:T(8,128)S(1)}) custom-call(s32[3]{0:T(128)S(1)} %pad_add_fusion.1.at_ref, bf16[16,416,128]{2,1,0:T(8,128)(2,1)} %constant_dynamic-update-slice_fusion.20.left_own, bf16[16,416,128]{2,1,0:T(8,128)(2,1)} %collective-permute-done.48.left_other, ...), custom_call_target="tpu_custom_call" | custom-call | flops 1 | bytes 1 | tf_op jit(solution)/shard_map/unpack/pallas_call | solution.py:536
  422.6 4.8 %convert_element_type.103 = f32[1600,1600]{1,0:T(8,128)} convert(bf16[1600,1600]{1,0:T(8,128)(2,1)S(1)} %copy-done.22) | non-fusion elementwise | flops 2560000 | bytes 15360000 | tf_op jit(solution)/shard_map/convert_element_type | solution.py:738
  427.4 9.7 %collective-permute-done.56.refs_1_ = bf16[208,1600]{1,0:T(8,128)(2,1)S(1)} collective-permute-done((bf16[208,1600]{1,0:T(8,128)(2,1)}, bf16[208,1600]{1,0:T(8,128)(2,1)S(1)}, u32[]{:S(2)}, u32[]{:S(2)}) %collective-permute-start.56) | collective-permute-done | bytes 665632 | tf_op jit(solution)/shard_map/ppermute | solution.py:583
  438.3 3.1 collective-permute-done.60.refs_5_
  445.2 5.8 %join_columns.1 = f32[400,6400]{1,0:T(8,128)} custom-call(s32[2]{0:T(128)S(1)} %copy-done.13, bf16[400,1600]{1,0:T(8,128)(2,1)S(1)} %constant_dynamic-slice_fusion.3.refs_0_, bf16[208,1600]{1,0:T(8,128)(2,1)S(1)} %collective-permute-done.56.refs_1_, bf16[208,1600]{1,0:T(8,128)(2,1)S(1)} %collective-permute-done.57.refs_2_, ...), custom_call_target="tpu_custom_call" | custom-call | flops 1 | bytes 1 | tf_op jit(solution)/shard_map/join_columns/pallas_call | solution.py:440
  (283 shorter events, 115.0 us)
Async XLA Ops:
  7.2 72.8 %all-gather.3.cloned.1.call-start = ((), (), s32[]{:S(2)}) async-start(), calls=%async_computation.5 | async-start | bytes 14057472 | tf_op jit(solution)/shard_map/all_gather | solution.py:610
  7.9 203.1 %all-gather.5.cloned.1.call-start = ((), (), s32[]{:S(2)}) async-start(), calls=%async_computation.6 | async-start | bytes 21086208 | tf_op jit(solution)/shard_map/all_gather | solution.py:654
  35.2 17.4 %collective-permute-start.3 = (bf16[208,1600]{1,0:T(8,128)(2,1)S(1)}, bf16[208,1600]{1,0:T(8,128)(2,1)}, u32[]{:S(2)}, u32[]{:S(2)}) collective-permute-start(bf16[208,1600]{1,0:T(8,128)(2,1)S(1)} %constant_dynamic-slice_fusion.13), channel_id=1, source_target_pairs={{1,0},{2,1},{3,2},{0,3},{5,4},{6,5},{7,6},{4,7},{9,8},{10,9},{11,1... | collective-permute-start | bytes 1996808 | tf_op jit(solution)/shard_map/ppermute | solution.py:583
  37.8 30.6 %collective-permute-start.5 = (bf16[208,1600]{1,0:T(8,128)(2,1)S(1)}, bf16[208,1600]{1,0:T(8,128)(2,1)}, u32[]{:S(2)}, u32[]{:S(2)}) collective-permute-start(bf16[208,1600]{1,0:T(8,128)(2,1)S(1)} %constant_dynamic-slice_fusion.13), channel_id=1, source_target_pairs={{2,0},{3,1},{0,2},{1,3},{6,4},{7,5},{4,6},{5,7},{10,8},{11,9},{8,1... | collective-permute-start | bytes 1996808 | tf_op jit(solution)/shard_map/ppermute | solution.py:583
  39.0 32.7 %collective-permute-start.7 = (bf16[208,1600]{1,0:T(8,128)(2,1)S(1)}, bf16[208,1600]{1,0:T(8,128)(2,1)}, u32[]{:S(2)}, u32[]{:S(2)}) collective-permute-start(bf16[208,1600]{1,0:T(8,128)(2,1)S(1)} %constant_dynamic-slice_fusion.13), channel_id=1, source_target_pairs={{3,0},{0,1},{1,2},{2,3},{7,4},{4,5},{5,6},{6,7},{11,8},{8,9},{9,10... | collective-permute-start | bytes 1996808 | tf_op jit(solution)/shard_map/ppermute | solution.py:583
  52.6 21.7 %collective-permute-start.4 = (bf16[208,1600]{1,0:T(8,128)(2,1)}, bf16[208,1600]{1,0:T(8,128)(2,1)}, u32[]{:S(2)}, u32[]{:S(2)}) collective-permute-start(bf16[208,1600]{1,0:T(8,128)(2,1)} %collective-permute-done.3.refs_1_), channel_id=1, source_target_pairs={{4,0},{0,4},{5,1},{1,5},{6,2},{2,6},{7,3},{3,7},{12,8},{8,12},{13,... | collective-permute-start | bytes 1996808 | tf_op jit(solution)/shard_map/ppermute | solution.py:583
  72.7 39.7 %collective-permute-start.12 = (bf16[208,1600]{1,0:T(8,128)(2,1)}, bf16[208,1600]{1,0:T(8,128)(2,1)}, u32[]{:S(2)}, u32[]{:S(2)}) collective-permute-start(bf16[208,1600]{1,0:T(8,128)(2,1)} %copy-done.18), channel_id=1, source_target_pairs={{1,0},{2,1},{3,2},{0,3},{5,4},{6,5},{7,6},{4,7},{9,8},{10,9},{11,1... | collective-permute-start | bytes 1996808 | tf_op jit(solution)/shard_map/ppermute | solution.py:583
  73.1 40.2 %collective-permute-start.13 = (bf16[208,1600]{1,0:T(8,128)(2,1)}, bf16[208,1600]{1,0:T(8,128)(2,1)}, u32[]{:S(2)}, u32[]{:S(2)}) collective-permute-start(bf16[208,1600]{1,0:T(8,128)(2,1)} %copy-done.17), channel_id=1, source_target_pairs={{2,0},{3,1},{0,2},{1,3},{6,4},{7,5},{4,6},{5,7},{10,8},{11,9},{8,1... | collective-permute-start | bytes 1996808 | tf_op jit(solution)/shard_map/ppermute | solution.py:583
  74.3 39.0 %collective-permute-start.14 = (bf16[208,1600]{1,0:T(8,128)(2,1)}, bf16[208,1600]{1,0:T(8,128)(2,1)}, u32[]{:S(2)}, u32[]{:S(2)}) collective-permute-start(bf16[208,1600]{1,0:T(8,128)(2,1)} %copy-done.16), channel_id=1, source_target_pairs={{3,0},{0,1},{1,2},{2,3},{7,4},{4,5},{5,6},{6,7},{11,8},{8,9},{9,10... | collective-permute-start | bytes 1996808 | tf_op jit(solution)/shard_map/ppermute | solution.py:583
  109.2 16.6 %collective-permute-start.15 = (bf16[128,1600]{1,0:T(8,128)(2,1)}, bf16[128,1600]{1,0:T(8,128)(2,1)}, u32[]{:S(2)}, u32[]{:S(2)}) collective-permute-start(bf16[128,1600]{1,0:T(8,128)(2,1)} %bitcast.15), channel_id=1, source_target_pairs={{1,0},{2,1},{3,2},{0,3},{5,4},{6,5},{7,6},{4,7},{9,8},{10,9},{11,1... | collective-permute-start | bytes 1228808 | tf_op jit(solution)/shard_map/ppermute | solution.py:583
  111.6 21.1 %collective-permute-start.16 = (bf16[128,1600]{1,0:T(8,128)(2,1)}, bf16[128,1600]{1,0:T(8,128)(2,1)}, u32[]{:S(2)}, u32[]{:S(2)}) collective-permute-start(bf16[128,1600]{1,0:T(8,128)(2,1)} %bitcast.15), channel_id=1, source_target_pairs={{2,0},{3,1},{0,2},{1,3},{6,4},{7,5},{4,6},{5,7},{10,8},{11,9},{8,1... | collective-permute-start | bytes 1228808 | tf_op jit(solution)/shard_map/ppermute | solution.py:583
  112.5 22.1 %collective-permute-start.17 = (bf16[128,1600]{1,0:T(8,128)(2,1)}, bf16[128,1600]{1,0:T(8,128)(2,1)}, u32[]{:S(2)}, u32[]{:S(2)}) collective-permute-start(bf16[128,1600]{1,0:T(8,128)(2,1)} %bitcast.15), channel_id=1, source_target_pairs={{3,0},{0,1},{1,2},{2,3},{7,4},{4,5},{5,6},{6,7},{11,8},{8,9},{9,10... | collective-permute-start | bytes 1228808 | tf_op jit(solution)/shard_map/ppermute | solution.py:583
  113.3 26.1 %all-to-all-start = ((bf16[32,64,128]{2,1,0:T(8,128)(2,1)}), bf16[32,64,128]{2,1,0:T(8,128)(2,1)}, u32[]{:S(2)}, u32[]{:S(2)}) async-start(bf16[32,64,128]{2,1,0:T(8,128)(2,1)} %get-tuple-element.82), calls=%async_computation | async-start | bytes 1048576 | tf_op jit(solution)/shard_map/all_to_all | solution.py:647
  123.3 278.3 %all-reduce.5.cloned.1.call-start = ((), (), s32[]{:S(2)}) async-start(), calls=%async_computation.7 | async-start | bytes 21299200 | tf_op jit(solution)/shard_map/psum | solution.py:676
  123.4 17.0 %collective-permute-start.18 = (bf16[208,1600]{1,0:T(8,128)(2,1)}, bf16[208,1600]{1,0:T(8,128)(2,1)S(1)}, u32[]{:S(2)}, u32[]{:S(2)}) collective-permute-start(bf16[208,1600]{1,0:T(8,128)(2,1)} %collective-permute-done.12.refs_1_), channel_id=1, source_target_pairs={{4,0},{0,4},{5,1},{1,5},{6,2},{2,6},{7,3},{3,7},{12,8},{8,12},{13,... | collective-permute-start | bytes 1996808 | tf_op jit(solution)/shard_map/ppermute | solution.py:583
  123.8 16.6 %collective-permute-start.19 = (bf16[208,1600]{1,0:T(8,128)(2,1)}, bf16[208,1600]{1,0:T(8,128)(2,1)S(1)}, u32[]{:S(2)}, u32[]{:S(2)}) collective-permute-start(bf16[208,1600]{1,0:T(8,128)(2,1)} %collective-permute-done.13.refs_3_), channel_id=1, source_target_pairs={{4,0},{0,4},{5,1},{1,5},{6,2},{2,6},{7,3},{3,7},{12,8},{8,12},{13,... | collective-permute-start | bytes 1996808 | tf_op jit(solution)/shard_map/ppermute | solution.py:583
  125.8 14.7 %collective-permute-start.20 = (bf16[208,1600]{1,0:T(8,128)(2,1)}, bf16[208,1600]{1,0:T(8,128)(2,1)}, u32[]{:S(2)}, u32[]{:S(2)}) collective-permute-start(bf16[208,1600]{1,0:T(8,128)(2,1)} %collective-permute-done.14.refs_5_), channel_id=1, source_target_pairs={{4,0},{0,4},{5,1},{1,5},{6,2},{2,6},{7,3},{3,7},{12,8},{8,12},{13,... | collective-permute-start | bytes 1996808 | tf_op jit(solution)/shard_map/ppermute | solution.py:583
  148.5 21.1 %collective-permute-start.23 = (bf16[128,1600]{1,0:T(8,128)(2,1)S(1)}, bf16[128,1600]{1,0:T(8,128)(2,1)S(1)}, u32[]{:S(2)}, u32[]{:S(2)}) collective-permute-start(bf16[128,1600]{1,0:T(8,128)(2,1)S(1)} %add_convert_fusion.1), channel_id=1, source_target_pairs={{3,0},{0,1},{1,2},{2,3},{7,4},{4,5},{5,6},{6,7},{11,8},{8,9},{9,10... | collective-permute-start | bytes 1228808 | tf_op jit(solution)/shard_map/ppermute | solution.py:583
  181.6 21.2 %collective-permute-start.24 = (bf16[128,1600]{1,0:T(8,128)(2,1)S(1)}, bf16[128,1600]{1,0:T(8,128)(2,1)S(1)}, u32[]{:S(2)}, u32[]{:S(2)}) collective-permute-start(bf16[128,1600]{1,0:T(8,128)(2,1)S(1)} %get-tuple-element.95), channel_id=1, source_target_pairs={{3,0},{0,1},{1,2},{2,3},{7,4},{4,5},{5,6},{6,7},{11,8},{8,9},{9,10... | collective-permute-start | bytes 1228808 | tf_op jit(solution)/shard_map/ppermute | solution.py:583
  181.6 29.4 %collective-permute-start.25 = (bf16[128,1600]{1,0:T(8,128)(2,1)}, bf16[128,1600]{1,0:T(8,128)(2,1)}, u32[]{:S(2)}, u32[]{:S(2)}) collective-permute-start(bf16[128,1600]{1,0:T(8,128)(2,1)} %get-tuple-element.96), channel_id=1, source_target_pairs={{2,0},{3,1},{0,2},{1,3},{6,4},{7,5},{4,6},{5,7},{10,8},{11,9},{8,1... | collective-permute-start | bytes 1228808 | tf_op jit(solution)/shard_map/ppermute | solution.py:583
  182.9 28.1 %collective-permute-start.26 = (bf16[128,1600]{1,0:T(8,128)(2,1)}, bf16[128,1600]{1,0:T(8,128)(2,1)}, u32[]{:S(2)}, u32[]{:S(2)}) collective-permute-start(bf16[128,1600]{1,0:T(8,128)(2,1)} %get-tuple-element.97), channel_id=1, source_target_pairs={{1,0},{2,1},{3,2},{0,3},{5,4},{6,5},{7,6},{4,7},{9,8},{10,9},{11,1... | collective-permute-start | bytes 1228808 | tf_op jit(solution)/shard_map/ppermute | solution.py:583
  220.2 24.0 %collective-permute-start.27 = (bf16[128,1600]{1,0:T(8,128)(2,1)}, bf16[128,1600]{1,0:T(8,128)(2,1)}, u32[]{:S(2)}, u32[]{:S(2)}) collective-permute-start(bf16[128,1600]{1,0:T(8,128)(2,1)} %get-tuple-element.105), channel_id=1, source_target_pairs={{1,0},{2,1},{3,2},{0,3},{5,4},{6,5},{7,6},{4,7},{9,8},{10,9},{11,1... | collective-permute-start | bytes 1228808 | tf_op jit(solution)/shard_map/ppermute | solution.py:583
  220.3 25.0 %collective-permute-start.28 = (bf16[128,1600]{1,0:T(8,128)(2,1)}, bf16[128,1600]{1,0:T(8,128)(2,1)S(1)}, u32[]{:S(2)}, u32[]{:S(2)}) collective-permute-start(bf16[128,1600]{1,0:T(8,128)(2,1)} %get-tuple-element.105), channel_id=1, source_target_pairs={{2,0},{3,1},{0,2},{1,3},{6,4},{7,5},{4,6},{5,7},{10,8},{11,9},{8,1... | collective-permute-start | bytes 1228808 | tf_op jit(solution)/shard_map/ppermute | solution.py:583
  221.1 16.2 %collective-permute-start.35 = (bf16[400,128]{1,0:T(8,128)(2,1)}, bf16[400,128]{1,0:T(8,128)(2,1)S(1)}, u32[]{:S(2)}, u32[]{:S(2)}) collective-permute-start(bf16[400,128]{1,0:T(8,128)(2,1)} %get-tuple-element.167), channel_id=1, source_target_pairs={{3,0},{0,1},{1,2},{2,3},{7,4},{4,5},{5,6},{6,7},{11,8},{8,9},{9,10... | collective-permute-start | bytes 307208 | tf_op jit(solution)/shard_map/ppermute | solution.py:583
  222.4 16.6 %collective-permute-start.34 = (bf16[400,128]{1,0:T(8,128)(2,1)S(1)}, bf16[400,128]{1,0:T(8,128)(2,1)S(1)}, u32[]{:S(2)}, u32[]{:S(2)}) collective-permute-start(bf16[400,128]{1,0:T(8,128)(2,1)S(1)} %get-tuple-element.168), channel_id=1, source_target_pairs={{2,0},{3,1},{0,2},{1,3},{6,4},{7,5},{4,6},{5,7},{10,8},{11,9},{8,1... | collective-permute-start | bytes 307208 | tf_op jit(solution)/shard_map/ppermute | solution.py:583
  226.1 18.0 %collective-permute-start.33 = (bf16[400,128]{1,0:T(8,128)(2,1)S(1)}, bf16[400,128]{1,0:T(8,128)(2,1)S(1)}, u32[]{:S(2)}, u32[]{:S(2)}) collective-permute-start(bf16[400,128]{1,0:T(8,128)(2,1)S(1)} %get-tuple-element.169), channel_id=1, source_target_pairs={{1,0},{2,1},{3,2},{0,3},{5,4},{6,5},{7,6},{4,7},{9,8},{10,9},{11,1... | collective-permute-start | bytes 307208 | tf_op jit(solution)/shard_map/ppermute | solution.py:583
  228.2 24.1 %all-to-all-start.1 = ((bf16[32,64,128]{2,1,0:T(8,128)(2,1)}), bf16[32,64,128]{2,1,0:T(8,128)(2,1)S(1)}, u32[]{:S(2)}, u32[]{:S(2)}) async-start(bf16[32,64,128]{2,1,0:T(8,128)(2,1)} %bitcast.17), calls=%async_computation.1 | async-start | bytes 1048576 | tf_op jit(solution)/shard_map/all_to_all | solution.py:683
  252.2 50.0 %all-to-all-start.4 = ((bf16[32,16,1600]{2,1,0:T(8,128)(2,1)}), bf16[32,16,1600]{2,1,0:T(8,128)(2,1)S(1)}, u32[]{:S(2)}, u32[]{:S(2)}) async-start(bf16[32,16,1600]{2,1,0:T(8,128)(2,1)} %out_grad.1), calls=%async_computation.4 | async-start | bytes 3407872 | tf_op jit(solution)/shard_map/all_to_all | solution.py:702
  260.3 25.3 %collective-permute-start.32 = (bf16[128,1600]{1,0:T(8,128)(2,1)}, bf16[128,1600]{1,0:T(8,128)(2,1)}, u32[]{:S(2)}, u32[]{:S(2)}) collective-permute-start(bf16[128,1600]{1,0:T(8,128)(2,1)} %get-tuple-element.108), channel_id=1, source_target_pairs={{1,0},{2,1},{3,2},{0,3},{5,4},{6,5},{7,6},{4,7},{9,8},{10,9},{11,1... | collective-permute-start | bytes 1228808 | tf_op jit(solution)/shard_map/ppermute | solution.py:583
  260.4 25.2 %collective-permute-start.31 = (bf16[128,1600]{1,0:T(8,128)(2,1)}, bf16[128,1600]{1,0:T(8,128)(2,1)}, u32[]{:S(2)}, u32[]{:S(2)}) collective-permute-start(bf16[128,1600]{1,0:T(8,128)(2,1)} %get-tuple-element.107), channel_id=1, source_target_pairs={{2,0},{3,1},{0,2},{1,3},{6,4},{7,5},{4,6},{5,7},{10,8},{11,9},{8,1... | collective-permute-start | bytes 1228808 | tf_op jit(solution)/shard_map/ppermute | solution.py:583
  262.6 23.0 %collective-permute-start.30 = (bf16[128,1600]{1,0:T(8,128)(2,1)}, bf16[128,1600]{1,0:T(8,128)(2,1)}, u32[]{:S(2)}, u32[]{:S(2)}) collective-permute-start(bf16[128,1600]{1,0:T(8,128)(2,1)} %get-tuple-element.106), channel_id=1, source_target_pairs={{3,0},{0,1},{1,2},{2,3},{7,4},{4,5},{5,6},{6,7},{11,8},{8,9},{9,10... | collective-permute-start | bytes 1228808 | tf_op jit(solution)/shard_map/ppermute | solution.py:583
  297.3 14.0 %collective-permute-start.39 = (bf16[416,192]{1,0:T(8,128)(2,1)}, bf16[416,192]{1,0:T(8,128)(2,1)S(1)}, u32[]{:S(2)}, u32[]{:S(2)}) collective-permute-start(bf16[416,192]{1,0:T(8,128)(2,1)} %get-tuple-element.121), channel_id=1, source_target_pairs={{1,0},{2,1},{3,2},{0,3},{5,4},{6,5},{7,6},{4,7},{9,8},{10,9},{11,1... | collective-permute-start | bytes 479240 | tf_op jit(solution)/shard_map/ppermute | solution.py:583
  302.3 74.6 %all-to-all-start.2 = ((bf16[32,192,128]{2,1,0:T(8,128)(2,1)}), bf16[32,192,128]{2,1,0:T(8,128)(2,1)S(1)}, u32[]{:S(2)}, u32[]{:S(2)}) async-start(bf16[32,192,128]{2,1,0:T(8,128)(2,1)} %get-tuple-element.114.grad_ref), calls=%async_computation.2 | async-start | bytes 3145728 | tf_op jit(solution)/shard_map/all_to_all | solution.py:705
  315.8 19.6 %collective-permute-start.42 = (bf16[416,128]{1,0:T(8,128)(2,1)S(1)}, bf16[416,128]{1,0:T(8,128)(2,1)S(1)}, u32[]{:S(2)}, u32[]{:S(2)}) collective-permute-start(bf16[416,128]{1,0:T(8,128)(2,1)S(1)} %get-tuple-element.124), channel_id=1, source_target_pairs={{8,0},{16,8},{24,16},{0,24},{9,1},{17,9},{25,17},{1,25},{10,2},{18... | collective-permute-start | bytes 319496 | tf_op jit(solution)/shard_map/ppermute | solution.py:583
  318.5 18.6 %collective-permute-start.43 = (bf16[416,128]{1,0:T(8,128)(2,1)S(1)}, bf16[416,128]{1,0:T(8,128)(2,1)S(1)}, u32[]{:S(2)}, u32[]{:S(2)}) collective-permute-start(bf16[416,128]{1,0:T(8,128)(2,1)S(1)} %get-tuple-element.124), channel_id=1, source_target_pairs={{16,0},{24,8},{0,16},{8,24},{17,1},{25,9},{1,17},{9,25},{18,2},{26... | collective-permute-start | bytes 319496 | tf_op jit(solution)/shard_map/ppermute | solution.py:583
  319.1 19.8 %collective-permute-start.44 = (bf16[416,128]{1,0:T(8,128)(2,1)S(1)}, bf16[416,128]{1,0:T(8,128)(2,1)S(1)}, u32[]{:S(2)}, u32[]{:S(2)}) collective-permute-start(bf16[416,128]{1,0:T(8,128)(2,1)S(1)} %get-tuple-element.124), channel_id=1, source_target_pairs={{24,0},{0,8},{8,16},{16,24},{25,1},{1,9},{9,17},{17,25},{26,2},{2,... | collective-permute-start | bytes 319496 | tf_op jit(solution)/shard_map/ppermute | solution.py:583
  321.2 20.8 %collective-permute-start.49 = (bf16[416,128]{1,0:T(8,128)(2,1)S(1)}, bf16[416,128]{1,0:T(8,128)(2,1)S(1)}, u32[]{:S(2)}, u32[]{:S(2)}) collective-permute-start(bf16[416,128]{1,0:T(8,128)(2,1)S(1)} %get-tuple-element.126), channel_id=1, source_target_pairs={{32,0},{64,32},{96,64},{0,96},{33,1},{65,33},{97,65},{1,97},{34,2}... | collective-permute-start | bytes 319496 | tf_op jit(solution)/shard_map/ppermute | solution.py:583
  323.6 18.8 %collective-permute-start.50 = (bf16[416,128]{1,0:T(8,128)(2,1)S(1)}, bf16[416,128]{1,0:T(8,128)(2,1)S(1)}, u32[]{:S(2)}, u32[]{:S(2)}) collective-permute-start(bf16[416,128]{1,0:T(8,128)(2,1)S(1)} %get-tuple-element.126), channel_id=1, source_target_pairs={{64,0},{96,32},{0,64},{32,96},{65,1},{97,33},{1,65},{33,97},{66,2}... | collective-permute-start | bytes 319496 | tf_op jit(solution)/shard_map/ppermute | solution.py:583
  342.0 25.8 %collective-permute-start.47 = (bf16[4,416,128]{2,1,0:T(8,128)(2,1)S(1)}, bf16[4,416,128]{2,1,0:T(8,128)(2,1)S(1)}, u32[]{:S(2)}, u32[]{:S(2)}) collective-permute-start(bf16[4,416,128]{2,1,0:T(8,128)(2,1)S(1)} %pad_maximum_fusion), channel_id=1, source_target_pairs={{96,0},{0,32},{32,64},{64,96},{97,1},{1,33},{33,65},{65,97},{98,2}... | collective-permute-start | bytes 1277960 | tf_op jit(solution)/shard_map/ppermute | solution.py:583
  342.4 26.7 %collective-permute-start.52 = (bf16[4,416,128]{2,1,0:T(8,128)(2,1)S(1)}, bf16[4,416,128]{2,1,0:T(8,128)(2,1)S(1)}, u32[]{:S(2)}, u32[]{:S(2)}) collective-permute-start(bf16[4,416,128]{2,1,0:T(8,128)(2,1)S(1)} %pad_maximum_fusion.1), channel_id=1, source_target_pairs={{8,0},{16,8},{24,16},{0,24},{9,1},{17,9},{25,17},{1,25},{10,2},{18... | collective-permute-start | bytes 1277960 | tf_op jit(solution)/shard_map/ppermute | solution.py:583
  345.4 24.5 %collective-permute-start.53 = (bf16[4,416,128]{2,1,0:T(8,128)(2,1)S(1)}, bf16[4,416,128]{2,1,0:T(8,128)(2,1)S(1)}, u32[]{:S(2)}, u32[]{:S(2)}) collective-permute-start(bf16[4,416,128]{2,1,0:T(8,128)(2,1)S(1)} %pad_maximum_fusion.1), channel_id=1, source_target_pairs={{16,0},{24,8},{0,16},{8,24},{17,1},{25,9},{1,17},{9,25},{18,2},{26... | collective-permute-start | bytes 1277960 | tf_op jit(solution)/shard_map/ppermute | solution.py:583
  350.7 20.0 %collective-permute-start.54 = (bf16[4,416,128]{2,1,0:T(8,128)(2,1)S(1)}, bf16[4,416,128]{2,1,0:T(8,128)(2,1)S(1)}, u32[]{:S(2)}, u32[]{:S(2)}) collective-permute-start(bf16[4,416,128]{2,1,0:T(8,128)(2,1)S(1)} %pad_maximum_fusion.1), channel_id=1, source_target_pairs={{24,0},{0,8},{8,16},{16,24},{25,1},{1,9},{9,17},{17,25},{26,2},{2,... | collective-permute-start | bytes 1277960 | tf_op jit(solution)/shard_map/ppermute | solution.py:583
  368.6 45.2 %collective-permute-start.48 = (bf16[16,416,128]{2,1,0:T(8,128)(2,1)}, bf16[16,416,128]{2,1,0:T(8,128)(2,1)}, u32[]{:S(2)}, u32[]{:S(2)}) collective-permute-start(bf16[16,416,128]{2,1,0:T(8,128)(2,1)} %constant_dynamic-update-slice_fusion.20.left_own), channel_id=1, source_target_pairs={{4,0},{0,4},{5,1},{1,5},{6,2},{2,6},{7,3},{3,7},{12,8},{8,12},{13,... | collective-permute-start | bytes 5111816 | tf_op jit(solution)/shard_map/ppermute | solution.py:583
  371.5 42.3 %collective-permute-start.55 = (bf16[16,416,128]{2,1,0:T(8,128)(2,1)}, bf16[16,416,128]{2,1,0:T(8,128)(2,1)}, u32[]{:S(2)}, u32[]{:S(2)}) collective-permute-start(bf16[16,416,128]{2,1,0:T(8,128)(2,1)} %constant_dynamic-update-slice_fusion.27.right_own), channel_id=1, source_target_pairs={{4,0},{0,4},{5,1},{1,5},{6,2},{2,6},{7,3},{3,7},{12,8},{8,12},{13,... | collective-permute-start | bytes 5111816 | tf_op jit(solution)/shard_map/ppermute | solution.py:583
  393.5 19.6 %all-to-all-start.3 = ((f32[32,8,400]{2,1,0:T(8,128)}), f32[32,8,400]{2,1,0:T(8,128)S(1)}, u32[]{:S(2)}, u32[]{:S(2)}) async-start(f32[32,8,400]{2,1,0:T(8,128)} %broadcast_in_dim.29), calls=%async_computation.3 | async-start | bytes 1048576 | tf_op jit(solution)/shard_map/all_to_all | solution.py:730
  404.5 32.6 %collective-permute-start.56 = (bf16[208,1600]{1,0:T(8,128)(2,1)}, bf16[208,1600]{1,0:T(8,128)(2,1)S(1)}, u32[]{:S(2)}, u32[]{:S(2)}) collective-permute-start(bf16[208,1600]{1,0:T(8,128)(2,1)} %get-tuple-element.154), channel_id=1, source_target_pairs={{1,0},{2,1},{3,2},{0,3},{5,4},{6,5},{7,6},{4,7},{9,8},{10,9},{11,1... | collective-permute-start | bytes 1996808 | tf_op jit(solution)/shard_map/ppermute | solution.py:583
  407.4 30.9 %collective-permute-start.58 = (bf16[208,1600]{1,0:T(8,128)(2,1)}, bf16[208,1600]{1,0:T(8,128)(2,1)S(1)}, u32[]{:S(2)}, u32[]{:S(2)}) collective-permute-start(bf16[208,1600]{1,0:T(8,128)(2,1)} %get-tuple-element.153), channel_id=1, source_target_pairs={{2,0},{3,1},{0,2},{1,3},{6,4},{7,5},{4,6},{5,7},{10,8},{11,9},{8,1... | collective-permute-start | bytes 1996808 | tf_op jit(solution)/shard_map/ppermute | solution.py:583
  407.7 33.7 %collective-permute-start.60 = (bf16[208,1600]{1,0:T(8,128)(2,1)S(1)}, bf16[208,1600]{1,0:T(8,128)(2,1)S(1)}, u32[]{:S(2)}, u32[]{:S(2)}) collective-permute-start(bf16[208,1600]{1,0:T(8,128)(2,1)S(1)} %get-tuple-element.152), channel_id=1, source_target_pairs={{3,0},{0,1},{1,2},{2,3},{7,4},{4,5},{5,6},{6,7},{11,8},{8,9},{9,10... | collective-permute-start | bytes 1996808 | tf_op jit(solution)/shard_map/ppermute | solution.py:583
  (54 other events, 494.5 us)
Sparse Core Ops, SparseCore 0:
  10.3 68.9 all-gather.2
  81.5 86.2 all-gather.4
  227.4 167.0 all-reduce.4

commit v2 on v1

--- a/solution.py
+++ b/solution.py
@@ -155,7 +155,7 @@
             jax.ShapeDtypeStruct((seqs, 1, length), F32),
         ],
         scratch_shapes=[pltpu.VMEM((seqs * length, HD), F32)],
-        compiler_params=pltpu.CompilerParams(vmem_limit_bytes=48 << 20),
+        compiler_params=pltpu.CompilerParams(vmem_limit_bytes=56 << 20),
         cost_estimate=pl.CostEstimate(
             flops=20_000_000_000, bytes_accessed=20_000_000, transcendentals=0
         ),
@@ -378,7 +378,7 @@
         in_specs=[pl.BlockSpec(memory_space=pltpu.SMEM)] + [vmem] * len(pieces),
         out_specs=vmem,
         out_shape=jax.ShapeDtypeStruct((n_w * own, width), BF),
-        compiler_params=pltpu.CompilerParams(vmem_limit_bytes=32 << 20),
+        compiler_params=pltpu.CompilerParams(vmem_limit_bytes=56 << 20),
         cost_estimate=pl.CostEstimate(flops=1, bytes_accessed=1, transcendentals=0),
         name="join_rows",
     )(at, *pieces)

time: 466 us -> 468 us (level)
  Pallas kernels: 93.5 us -> 101 us
  waiting for transfers between devices: 106 us -> 101 us
    ppermute x62, waiting for transfers between devices: 99.9 us -> 93.6 us  [shift(): return lax.ppermute(array, axis, [((i + k) % size, i) for i in range(size)])]
    pallas_call x2, Pallas kernels: 4.78 us -> 10.7 us  [join_rows(): pl.pallas_call(functools.partial(join_rows_kernel, n_w, overlap), in_spec...]
    unnamed x98 -> x112, local copies, waits for them, and re-layouts: 30.4 us -> 27.1 us
  transfers between devices with their start and end apart: 70 -> 70, of which waited for: 21 -> 22; matrix products, arithmetic and copies ran while one was open for 18% -> 20% of each run, Pallas kernels for 19% -> 21%
where the time goes in v2:
time: 468 us; the launch traced here: 460 us
  starting transfers between devices  137 us (29%)
  waiting for transfers between devices  101 us (22%)
  Pallas kernels  101 us (22%)
  local copies, waits for them, and re-layouts  48.1 us (10%)
  matrix products  43.3 us (9%)
  between operations  15.1 us (3%)
  other arithmetic  14.9 us (3%)
    ppermute x62, waiting for transfers between devices, shift(): return lax.ppermute(array, axis, [((i + k) % size, i) for i in range(size)])  93.6 us
    ppermute x62, starting transfers between devices, shift(): return lax.ppermute(array, axis, [((i + k) % size, i) for i in range(size)])  92 us
    dot_general x8, matrix products, mm(): return lax.dot_general(left, right, dims, preferred_element_type=F32)  43.3 us
    pallas_call x1, Pallas kernels, attend(): pl.pallas_call(functools.partial(attend_kernel, seqs, rows, half), grid=(...  28 us
    unnamed x112, local copies, waits for them, and re-layouts  27.1 us
    pallas_call x1, Pallas kernels, attend_back(): pl.pallas_call(functools.partial(attend_back_kernel, seqs, rows, half), i...  21.3 us
    pallas_call x1, Pallas kernels, head_grad(): pl.pallas_call(functools.partial(head_grad_kernel, n_w), grid=(n_ctx // g...  11.2 us
    pallas_call x2, Pallas kernels, join_rows(): pl.pallas_call(functools.partial(join_rows_kernel, n_w, overlap), in_spec...  10.7 us
  transfers between devices with their start and end apart: 70, of which 22 were waited for; matrix products, arithmetic and copies ran while one was open for 20% of the time, Pallas kernels for 21%

profile of v2, /device:TPU:1, one launch (start us, length us, event | category | flops | bytes accessed | tf_op | source)
XLA Modules:
  0.0 460.1 jit_solution(15925850238039461002)
XLA Ops:
  9.3 3.4 collective-permute-start
  13.8 3.8 collective-permute-done
  19.8 5.7 %collective-permute-done.2 = bf16[400,192]{1,0:T(8,128)(2,1)S(1)} collective-permute-done((bf16[400,192]{1,0:T(8,128)(2,1)S(1)}, bf16[400,192]{1,0:T(8,128)(2,1)S(1)}, u32[]{:S(2)}, u32[]{:S(2)}) %collective-permute-start.2) | collective-permute-done | bytes 153632 | tf_op jit(solution)/shard_map/ppermute | solution.py:583
  43.8 10.3 %collective-permute-done.3.refs_1_ = bf16[208,1600]{1,0:T(8,128)(2,1)} collective-permute-done((bf16[208,1600]{1,0:T(8,128)(2,1)S(1)}, bf16[208,1600]{1,0:T(8,128)(2,1)}, u32[]{:S(2)}, u32[]{:S(2)}) %collective-permute-start.3) | collective-permute-done | bytes 665632 | tf_op jit(solution)/shard_map/ppermute | solution.py:583
  54.1 15.8 %collective-permute-start.4 = (bf16[208,1600]{1,0:T(8,128)(2,1)}, bf16[208,1600]{1,0:T(8,128)(2,1)}, u32[]{:S(2)}, u32[]{:S(2)}) collective-permute-start(bf16[208,1600]{1,0:T(8,128)(2,1)} %collective-permute-done.3.refs_1_), channel_id=1, source_target_pairs={{4,0},{0,4},{5,1},{1,5},{6,2},{2,6},{7,3},{3,7},{12,8},{8,12},{13,... | collective-permute-start | bytes 1996808 | tf_op jit(solution)/shard_map/ppermute | solution.py:583
  69.9 3.3 collective-permute-done.7.refs_5_
  78.1 5.3 %join_rows.2 = bf16[1600,1600]{1,0:T(8,128)(2,1)} custom-call(s32[2]{0:T(128)} %copy-done.11, bf16[400,1600]{1,0:T(8,128)(2,1)} %refs_0_.1, bf16[208,1600]{1,0:T(8,128)(2,1)} %collective-permute-done.3.refs_1_, bf16[208,1600]{1,0:T(8,128)(2,1)} %collective-permute-done.4.refs_2_, bf16[208,1600]{1,0:T(8,128)(2,1)} %collective-permute-done.5.refs_3_, ...), custom_call_target="tpu_custom_call" | custom-call | flops 1 | bytes 1 | tf_op jit(solution)/shard_map/join_rows/pallas_call | solution.py:376
  83.5 28.0 %attend.1 = (bf16[4096,1600]{1,0:T(8,128)(2,1)}, bf16[4096,192]{1,0:T(8,128)(2,1)}, bf16[32,64,128]{2,1,0:T(8,128)(2,1)}, f32[2,64,2048]{2,1,0:T(8,128)}, f32[2,1,2048]{2,1,0:T(1,128)}) custom-call(s32[2,64]{1,0:T(2,128)} %order_ref.3, bf16[4096,1600]{1,0:T(8,128)(2,1)} %all-gather.3.cloned.1.call-done.in_ref, f32[1,1600]{1,0:T(1,128)} %slice.109.gain_ref, ...), custom_call_target="tpu_custom_call" | custom-call | flops 20000000000 | bytes 20000000 | tf_op jit(solution)/shard_map/attend/pallas_call | solution.py:132
  115.8 9.8 %all-to-all-start = ((bf16[32,64,128]{2,1,0:T(8,128)(2,1)}), bf16[32,64,128]{2,1,0:T(8,128)(2,1)S(1)}, u32[]{:S(2)}, u32[]{:S(2)}) async-start(bf16[32,64,128]{2,1,0:T(8,128)(2,1)} %get-tuple-element.82), calls=%async_computation | async-start | bytes 1048576 | tf_op jit(solution)/shard_map/all_to_all | solution.py:647
  127.0 5.9 %collective-permute-start.20 = (bf16[208,1600]{1,0:T(8,128)(2,1)}, bf16[208,1600]{1,0:T(8,128)(2,1)}, u32[]{:S(2)}, u32[]{:S(2)}) collective-permute-start(bf16[208,1600]{1,0:T(8,128)(2,1)} %collective-permute-done.14.refs_5_), channel_id=1, source_target_pairs={{4,0},{0,4},{5,1},{1,5},{6,2},{2,6},{7,3},{3,7},{12,8},{8,12},{13,... | collective-permute-start | bytes 1996808 | tf_op jit(solution)/shard_map/ppermute | solution.py:583
  138.3 3.2 all-to-all-done
  142.4 3.7 fusion.8
  149.7 5.7 %fusion.11 = f32[512,1600]{0,1:T(8,128)S(1)} fusion(bf16[512,1600]{1,0:T(8,128)(2,1)} %constant_dynamic-update-slice_fusion.8, bf16[1600,1600]{1,0:T(8,128)(2,1)} %param.23), kind=kOutput, calls=%fused_computation.115 | convolution fusion | flops 2621440000 | bytes 10035200 | tf_op jit(solution)/shard_map/dot_general | solution.py:24
  155.4 5.4 %join_rows.3 = bf16[1600,1600]{1,0:T(8,128)(2,1)} custom-call(s32[2]{0:T(128)} %copy-done.11, bf16[400,1600]{1,0:T(8,128)(2,1)} %copy-done.5, bf16[208,1600]{1,0:T(8,128)(2,1)} %copy-done.23, bf16[208,1600]{1,0:T(8,128)(2,1)} %copy-done.24, bf16[208,1600]{1,0:T(8,128)(2,1)} %collective-permute-done.13.refs_3_, ...), custom_call_target="tpu_custom_call" | custom-call | flops 1 | bytes 1 | tf_op jit(solution)/shard_map/join_rows/pallas_call | solution.py:376
  160.8 10.1 %collective-permute-done.23 = bf16[128,1600]{1,0:T(8,128)(2,1)S(1)} collective-permute-done((bf16[128,1600]{1,0:T(8,128)(2,1)S(1)}, bf16[128,1600]{1,0:T(8,128)(2,1)S(1)}, u32[]{:S(2)}, u32[]{:S(2)}) %collective-permute-start.23) | collective-permute-done | bytes 409632 | tf_op jit(solution)/shard_map/ppermute | solution.py:583
  171.0 5.9 %convolution_add_fusion = f32[512,1600]{0,1:T(8,128)S(1)} fusion(bf16[512,1600]{1,0:T(8,128)(2,1)S(1)} %constant_dynamic-update-slice_fusion.12, bf16[1600,1600]{1,0:T(8,128)(2,1)} %join_rows.3, f32[1600]{0:T(1024)S(1)} %convert_element_type.85), kind=kOutput, calls=%fused_computation.8 | convolution fusion | flops 2622259200 | bytes 10041600 | tf_op jit(solution)/shard_map/dot_general | solution.py:24
  179.2 5.3 %fusion.9 = (bf16[512,1600]{1,0:T(8,128)(2,1)S(1)}, f32[512,1600]{1,0:T(8,128)}) fusion(bf16[512,1600]{0,1:T(8,128)(2,1)S(1)} %get-tuple-element.100, bf16[1600,1600]{1,0:T(8,128)(2,1)S(1)} %bitcast.85), kind=kOutput, calls=%fused_computation.113 | convolution fusion | flops 2622259200 | bytes 11673600 | tf_op jit(solution)/shard_map/dot_general | solution.py:24
  189.3 5.7 %convolution_convert_fusion = bf16[1600,1600]{1,0:T(8,128)(2,1)} fusion(bf16[512,1600]{1,0:T(8,128)(2,1)S(1)} %constant_dynamic-update-slice_fusion.12, bf16[512,1600]{0,1:T(8,128)(2,1)S(1)} %get-tuple-element.100), kind=kOutput, calls=%fused_computation | convolution fusion | flops 2624000000 | bytes 8396800 | tf_op jit(solution)/shard_map/dot_general | solution.py:24
  195.0 6.3 %convolution_convert_fusion.1 = bf16[1600,1600]{1,0:T(8,128)(2,1)} fusion(bf16[512,1600]{0,1:T(8,128)(2,1)S(1)} %get-tuple-element.99, bf16[512,1600]{1,0:T(8,128)(2,1)} %constant_dynamic-update-slice_fusion.8), kind=kOutput, calls=%fused_computation.1 | convolution fusion | flops 2624000000 | bytes 8396800 | tf_op jit(solution)/shard_map/dot_general | solution.py:24
  201.3 5.7 %collective-permute-done.24 = bf16[128,1600]{1,0:T(8,128)(2,1)S(1)} collective-permute-done((bf16[128,1600]{1,0:T(8,128)(2,1)}, bf16[128,1600]{1,0:T(8,128)(2,1)S(1)}, u32[]{:S(2)}, u32[]{:S(2)}) %collective-permute-start.24) | collective-permute-done | bytes 409632 | tf_op jit(solution)/shard_map/ppermute | solution.py:583
  207.0 6.6 %fusion.10 = (bf16[512,1600]{1,0:T(8,128)(2,1)S(1)}, f32[512,1600]{1,0:T(8,128)S(1)}) fusion(bf16[512,1600]{0,1:T(8,128)(2,1)} %copy-done.17, bf16[1600,1600]{1,0:T(8,128)(2,1)} %param.23), kind=kOutput, calls=%fused_computation.114 | convolution fusion | flops 2622259200 | bytes 11673600 | tf_op jit(solution)/shard_map/dot_general | solution.py:24
  218.8 4.1 convolution_convert_fusion.2
  225.2 3.7 collective-permute-start.34
  229.9 9.5 %all-to-all-start.1 = ((bf16[32,64,128]{2,1,0:T(8,128)(2,1)}), bf16[32,64,128]{2,1,0:T(8,128)(2,1)S(1)}, u32[]{:S(2)}, u32[]{:S(2)}) async-start(bf16[32,64,128]{2,1,0:T(8,128)(2,1)} %bitcast.95), calls=%async_computation.1 | async-start | bytes 1048576 | tf_op jit(solution)/shard_map/all_to_all | solution.py:683
  241.1 5.5 %collective-permute-done.33 = bf16[400,128]{1,0:T(8,128)(2,1)} collective-permute-done((bf16[400,128]{1,0:T(8,128)(2,1)}, bf16[400,128]{1,0:T(8,128)(2,1)}, u32[]{:S(2)}, u32[]{:S(2)}) %collective-permute-start.33) | collective-permute-done | bytes 102432 | tf_op jit(solution)/shard_map/ppermute | solution.py:583
  248.8 3.1 collective-permute-done.29
  254.0 8.4 %all-to-all-start.4 = ((bf16[32,16,1600]{2,1,0:T(8,128)(2,1)}), bf16[32,16,1600]{2,1,0:T(8,128)(2,1)S(1)}, u32[]{:S(2)}, u32[]{:S(2)}) async-start(bf16[32,16,1600]{2,1,0:T(8,128)(2,1)} %out_grad.1), calls=%async_computation.4 | async-start | bytes 3407872 | tf_op jit(solution)/shard_map/all_to_all | solution.py:702
  266.2 21.3 %attend_back.1 = (bf16[32,192,128]{2,1,0:T(8,128)(2,1)}, f32[1,192]{1,0:T(1,128)S(1)}) custom-call(s32[2,64]{1,0:T(2,128)S(1)} %copy-done.14, bf16[4096,192]{1,0:T(8,128)(2,1)S(1)} %copy-done.4, f32[2,64,2048]{2,1,0:T(8,128)S(1)} %copy-done.6, f32[2,1,2048]{2,1,0:T(1,128)S(1)} %copy-done.10, bf16[32,64,128]{2,1,0:T(8,128)(2,1)S(1)} %all-to-all-done.1.grad_ref), custom_call_target="tpu_custom_call" | custom-call | flops 1 | bytes 1 | tf_op jit(solution)/shard_map/attend_back/pallas_call | solution.py:240
  289.1 11.2 %head_grad.1 = (f32[416,192]{1,0:T(8,128)}, bf16[416,192]{1,0:T(8,128)(2,1)}, bf16[416,192]{1,0:T(8,128)(2,1)}, bf16[416,192]{1,0:T(8,128)(2,1)}) custom-call(s32[2]{0:T(128)} %copy-done.11, bf16[32,192,128]{2,1,0:T(8,128)(2,1)} %get-tuple-element.114.grad_ref, f32[1,192]{1,0:T(1,128)} %copy-done.13, bf16[4096,1600]{1,0:T(8,128)(2,1)} %get-tuple-element.119.in_ref), custom_call_target="tpu_custom_call" | custom-call | flops 1 | bytes 1 | tf_op jit(solution)/shard_map/head_grad/pallas_call | solution.py:288
  300.3 2.7 collective-permute-start.39
  304.4 9.1 %all-to-all-start.2 = ((bf16[32,192,128]{2,1,0:T(8,128)(2,1)}), bf16[32,192,128]{2,1,0:T(8,128)(2,1)S(1)}, u32[]{:S(2)}, u32[]{:S(2)}) async-start(bf16[32,192,128]{2,1,0:T(8,128)(2,1)} %get-tuple-element.114.grad_ref), calls=%async_computation.2 | async-start | bytes 3145728 | tf_op jit(solution)/shard_map/all_to_all | solution.py:705
  313.6 3.1 collective-permute-done.41.refs_3_
  319.1 2.7 collective-permute-start.42
  327.1 10.6 %collective-permute-done.42 = bf16[416,128]{1,0:T(8,128)(2,1)S(1)} collective-permute-done((bf16[416,128]{1,0:T(8,128)(2,1)S(1)}, bf16[416,128]{1,0:T(8,128)(2,1)S(1)}, u32[]{:S(2)}, u32[]{:S(2)}) %collective-permute-start.42) | collective-permute-done | bytes 106528 | tf_op jit(solution)/shard_map/ppermute | solution.py:583
  341.2 2.7 collective-permute-start.45
  344.9 2.9 collective-permute-start.52
  356.7 13.3 %collective-permute-done.47 = bf16[4,416,128]{2,1,0:T(8,128)(2,1)S(1)} collective-permute-done((bf16[4,416,128]{2,1,0:T(8,128)(2,1)S(1)}, bf16[4,416,128]{2,1,0:T(8,128)(2,1)S(1)}, u32[]{:S(2)}, u32[]{:S(2)}) %collective-permute-start.47) | collective-permute-done | bytes 426016 | tf_op jit(solution)/shard_map/ppermute | solution.py:583
  373.7 6.1 %collective-permute-start.55 = (bf16[16,416,128]{2,1,0:T(8,128)(2,1)}, bf16[16,416,128]{2,1,0:T(8,128)(2,1)}, u32[]{:S(2)}, u32[]{:S(2)}) collective-permute-start(bf16[16,416,128]{2,1,0:T(8,128)(2,1)} %constant_dynamic-update-slice_fusion.27.right_own), channel_id=1, source_target_pairs={{4,0},{0,4},{5,1},{1,5},{6,2},{2,6},{7,3},{3,7},{12,8},{8,12},{13,... | collective-permute-start | bytes 5111816 | tf_op jit(solution)/shard_map/ppermute | solution.py:583
  379.9 10.0 %finish.1 = (f32[128,1600]{1,0:T(8,128)}, f32[4,8,400]{2,1,0:T(8,128)S(1)}) custom-call(bf16[6144,128]{1,0:T(8,128)(2,1)S(1)} %bitcast.78, bf16[6144,1600]{1,0:T(8,128)(2,1)} %all-gather.5.cloned.1.call-done.weight_ref, bf16[128,1600]{1,0:T(8,128)(2,1)S(1)} %bitcast.81, f32[1,1600]{1,0:T(1,128)S(1)} %copy-done.8, f32[1,1600]{1,0:T(1,128)S(1)} %copy-done.9, ...), custom_call_target="tpu_custom_call" | custom-call | flops 1 | bytes 1 | tf_op jit(solution)/shard_map/finish/pallas_call | solution.py:336
  395.5 8.2 %all-to-all-start.3 = ((f32[32,8,400]{2,1,0:T(8,128)}), f32[32,8,400]{2,1,0:T(8,128)S(1)}, u32[]{:S(2)}, u32[]{:S(2)}) async-start(f32[32,8,400]{2,1,0:T(8,128)} %broadcast_in_dim.29), calls=%async_computation.3 | async-start | bytes 1048576 | tf_op jit(solution)/shard_map/all_to_all | solution.py:730
  403.7 2.9 constant_dynamic-slice_fusion
  406.7 2.8 collective-permute-start.56
  411.8 3.4 all-to-all-done.3
  415.9 8.8 %unpack.1 = (f32[400,4800]{1,0:T(8,128)}, f32[400,1600]{1,0:T(8,128)}, f32[8,1600]{1,0:T(8,128)S(1)}, f32[8,1600]{1,0:T(8,128)S(1)}) custom-call(s32[3]{0:T(128)S(1)} %pad_add_fusion.1.at_ref, bf16[16,416,128]{2,1,0:T(8,128)(2,1)} %constant_dynamic-update-slice_fusion.20.left_own, bf16[16,416,128]{2,1,0:T(8,128)(2,1)} %collective-permute-done.48.left_other, ...), custom_call_target="tpu_custom_call" | custom-call | flops 1 | bytes 1 | tf_op jit(solution)/shard_map/unpack/pallas_call | solution.py:536
  424.7 4.8 %convert_element_type.103 = f32[1600,1600]{1,0:T(8,128)} convert(bf16[1600,1600]{1,0:T(8,128)(2,1)S(1)} %copy-done.18) | non-fusion elementwise | flops 2560000 | bytes 15360000 | tf_op jit(solution)/shard_map/convert_element_type | solution.py:738
  429.5 9.6 %collective-permute-done.56.refs_1_ = bf16[208,1600]{1,0:T(8,128)(2,1)S(1)} collective-permute-done((bf16[208,1600]{1,0:T(8,128)(2,1)}, bf16[208,1600]{1,0:T(8,128)(2,1)S(1)}, u32[]{:S(2)}, u32[]{:S(2)}) %collective-permute-start.56) | collective-permute-done | bytes 665632 | tf_op jit(solution)/shard_map/ppermute | solution.py:583
  440.3 3.1 collective-permute-done.60.refs_5_
  447.3 5.8 %join_columns.1 = f32[400,6400]{1,0:T(8,128)} custom-call(s32[2]{0:T(128)S(1)} %copy-done.12, bf16[400,1600]{1,0:T(8,128)(2,1)S(1)} %constant_dynamic-slice_fusion.3.refs_0_, bf16[208,1600]{1,0:T(8,128)(2,1)S(1)} %collective-permute-done.56.refs_1_, bf16[208,1600]{1,0:T(8,128)(2,1)S(1)} %collective-permute-done.57.refs_2_, ...), custom_call_target="tpu_custom_call" | custom-call | flops 1 | bytes 1 | tf_op jit(solution)/shard_map/join_columns/pallas_call | solution.py:440
  (298 shorter events, 110.7 us)
Async XLA Ops:
  7.2 76.3 %all-gather.3.cloned.1.call-start = ((), (), s32[]{:S(2)}) async-start(), calls=%async_computation.5 | async-start | bytes 14057472 | tf_op jit(solution)/shard_map/all_gather | solution.py:610
  7.9 207.8 %all-gather.5.cloned.1.call-start = ((), (), s32[]{:S(2)}) async-start(), calls=%async_computation.6 | async-start | bytes 21086208 | tf_op jit(solution)/shard_map/all_gather | solution.py:654
  36.7 17.4 %collective-permute-start.3 = (bf16[208,1600]{1,0:T(8,128)(2,1)S(1)}, bf16[208,1600]{1,0:T(8,128)(2,1)}, u32[]{:S(2)}, u32[]{:S(2)}) collective-permute-start(bf16[208,1600]{1,0:T(8,128)(2,1)S(1)} %constant_dynamic-slice_fusion.13), channel_id=1, source_target_pairs={{1,0},{2,1},{3,2},{0,3},{5,4},{6,5},{7,6},{4,7},{9,8},{10,9},{11,1... | collective-permute-start | bytes 1996808 | tf_op jit(solution)/shard_map/ppermute | solution.py:583
  39.3 30.6 %collective-permute-start.5 = (bf16[208,1600]{1,0:T(8,128)(2,1)S(1)}, bf16[208,1600]{1,0:T(8,128)(2,1)}, u32[]{:S(2)}, u32[]{:S(2)}) collective-permute-start(bf16[208,1600]{1,0:T(8,128)(2,1)S(1)} %constant_dynamic-slice_fusion.13), channel_id=1, source_target_pairs={{2,0},{3,1},{0,2},{1,3},{6,4},{7,5},{4,6},{5,7},{10,8},{11,9},{8,1... | collective-permute-start | bytes 1996808 | tf_op jit(solution)/shard_map/ppermute | solution.py:583
  40.4 32.8 %collective-permute-start.7 = (bf16[208,1600]{1,0:T(8,128)(2,1)S(1)}, bf16[208,1600]{1,0:T(8,128)(2,1)}, u32[]{:S(2)}, u32[]{:S(2)}) collective-permute-start(bf16[208,1600]{1,0:T(8,128)(2,1)S(1)} %constant_dynamic-slice_fusion.13), channel_id=1, source_target_pairs={{3,0},{0,1},{1,2},{2,3},{7,4},{4,5},{5,6},{6,7},{11,8},{8,9},{9,10... | collective-permute-start | bytes 1996808 | tf_op jit(solution)/shard_map/ppermute | solution.py:583
  54.1 23.3 %collective-permute-start.4 = (bf16[208,1600]{1,0:T(8,128)(2,1)}, bf16[208,1600]{1,0:T(8,128)(2,1)}, u32[]{:S(2)}, u32[]{:S(2)}) collective-permute-start(bf16[208,1600]{1,0:T(8,128)(2,1)} %collective-permute-done.3.refs_1_), channel_id=1, source_target_pairs={{4,0},{0,4},{5,1},{1,5},{6,2},{2,6},{7,3},{3,7},{12,8},{8,12},{13,... | collective-permute-start | bytes 1996808 | tf_op jit(solution)/shard_map/ppermute | solution.py:583
  76.0 39.0 %collective-permute-start.12 = (bf16[208,1600]{1,0:T(8,128)(2,1)S(1)}, bf16[208,1600]{1,0:T(8,128)(2,1)S(1)}, u32[]{:S(2)}, u32[]{:S(2)}) collective-permute-start(bf16[208,1600]{1,0:T(8,128)(2,1)S(1)} %get-tuple-element.77), channel_id=1, source_target_pairs={{1,0},{2,1},{3,2},{0,3},{5,4},{6,5},{7,6},{4,7},{9,8},{10,9},{11,1... | collective-permute-start | bytes 1996808 | tf_op jit(solution)/shard_map/ppermute | solution.py:583
  76.3 39.4 %collective-permute-start.13 = (bf16[208,1600]{1,0:T(8,128)(2,1)S(1)}, bf16[208,1600]{1,0:T(8,128)(2,1)}, u32[]{:S(2)}, u32[]{:S(2)}) collective-permute-start(bf16[208,1600]{1,0:T(8,128)(2,1)S(1)} %get-tuple-element.79), channel_id=1, source_target_pairs={{2,0},{3,1},{0,2},{1,3},{6,4},{7,5},{4,6},{5,7},{10,8},{11,9},{8,1... | collective-permute-start | bytes 1996808 | tf_op jit(solution)/shard_map/ppermute | solution.py:583
  77.4 38.3 %collective-permute-start.14 = (bf16[208,1600]{1,0:T(8,128)(2,1)S(1)}, bf16[208,1600]{1,0:T(8,128)(2,1)}, u32[]{:S(2)}, u32[]{:S(2)}) collective-permute-start(bf16[208,1600]{1,0:T(8,128)(2,1)S(1)} %get-tuple-element.81), channel_id=1, source_target_pairs={{3,0},{0,1},{1,2},{2,3},{7,4},{4,5},{5,6},{6,7},{11,8},{8,9},{9,10... | collective-permute-start | bytes 1996808 | tf_op jit(solution)/shard_map/ppermute | solution.py:583
  111.5 15.5 %collective-permute-start.15 = (bf16[128,1600]{1,0:T(8,128)(2,1)S(1)}, bf16[128,1600]{1,0:T(8,128)(2,1)}, u32[]{:S(2)}, u32[]{:S(2)}) collective-permute-start(bf16[128,1600]{1,0:T(8,128)(2,1)S(1)} %bitcast.86), channel_id=1, source_target_pairs={{1,0},{2,1},{3,2},{0,3},{5,4},{6,5},{7,6},{4,7},{9,8},{10,9},{11,1... | collective-permute-start | bytes 1228808 | tf_op jit(solution)/shard_map/ppermute | solution.py:583
  113.9 20.7 %collective-permute-start.16 = (bf16[128,1600]{1,0:T(8,128)(2,1)S(1)}, bf16[128,1600]{1,0:T(8,128)(2,1)}, u32[]{:S(2)}, u32[]{:S(2)}) collective-permute-start(bf16[128,1600]{1,0:T(8,128)(2,1)S(1)} %bitcast.87), channel_id=1, source_target_pairs={{2,0},{3,1},{0,2},{1,3},{6,4},{7,5},{4,6},{5,7},{10,8},{11,9},{8,1... | collective-permute-start | bytes 1228808 | tf_op jit(solution)/shard_map/ppermute | solution.py:583
  115.0 21.5 %collective-permute-start.17 = (bf16[128,1600]{1,0:T(8,128)(2,1)S(1)}, bf16[128,1600]{1,0:T(8,128)(2,1)}, u32[]{:S(2)}, u32[]{:S(2)}) collective-permute-start(bf16[128,1600]{1,0:T(8,128)(2,1)S(1)} %bitcast.88), channel_id=1, source_target_pairs={{3,0},{0,1},{1,2},{2,3},{7,4},{4,5},{5,6},{6,7},{11,8},{8,9},{9,10... | collective-permute-start | bytes 1228808 | tf_op jit(solution)/shard_map/ppermute | solution.py:583
  115.8 25.8 %all-to-all-start = ((bf16[32,64,128]{2,1,0:T(8,128)(2,1)}), bf16[32,64,128]{2,1,0:T(8,128)(2,1)S(1)}, u32[]{:S(2)}, u32[]{:S(2)}) async-start(bf16[32,64,128]{2,1,0:T(8,128)(2,1)} %get-tuple-element.82), calls=%async_computation | async-start | bytes 1048576 | tf_op jit(solution)/shard_map/all_to_all | solution.py:647
  125.5 278.1 %all-reduce.5.cloned.1.call-start = ((), (), s32[]{:S(2)}) async-start(), calls=%async_computation.7 | async-start | bytes 21299200 | tf_op jit(solution)/shard_map/psum | solution.py:676
  125.6 16.0 %collective-permute-start.18 = (bf16[208,1600]{1,0:T(8,128)(2,1)S(1)}, bf16[208,1600]{1,0:T(8,128)(2,1)S(1)}, u32[]{:S(2)}, u32[]{:S(2)}) collective-permute-start(bf16[208,1600]{1,0:T(8,128)(2,1)S(1)} %collective-permute-done.12.refs_1_), channel_id=1, source_target_pairs={{4,0},{0,4},{5,1},{1,5},{6,2},{2,6},{7,3},{3,7},{12,8},{8,12},{13,... | collective-permute-start | bytes 1996808 | tf_op jit(solution)/shard_map/ppermute | solution.py:583
  125.9 15.7 %collective-permute-start.19 = (bf16[208,1600]{1,0:T(8,128)(2,1)}, bf16[208,1600]{1,0:T(8,128)(2,1)}, u32[]{:S(2)}, u32[]{:S(2)}) collective-permute-start(bf16[208,1600]{1,0:T(8,128)(2,1)} %collective-permute-done.13.refs_3_), channel_id=1, source_target_pairs={{4,0},{0,4},{5,1},{1,5},{6,2},{2,6},{7,3},{3,7},{12,8},{8,12},{13,... | collective-permute-start | bytes 1996808 | tf_op jit(solution)/shard_map/ppermute | solution.py:583
  127.0 14.6 %collective-permute-start.20 = (bf16[208,1600]{1,0:T(8,128)(2,1)}, bf16[208,1600]{1,0:T(8,128)(2,1)}, u32[]{:S(2)}, u32[]{:S(2)}) collective-permute-start(bf16[208,1600]{1,0:T(8,128)(2,1)} %collective-permute-done.14.refs_5_), channel_id=1, source_target_pairs={{4,0},{0,4},{5,1},{1,5},{6,2},{2,6},{7,3},{3,7},{12,8},{8,12},{13,... | collective-permute-start | bytes 1996808 | tf_op jit(solution)/shard_map/ppermute | solution.py:583
  146.6 14.1 %collective-permute-start.21 = (bf16[128,1600]{1,0:T(8,128)(2,1)S(1)}, bf16[128,1600]{1,0:T(8,128)(2,1)S(1)}, u32[]{:S(2)}, u32[]{:S(2)}) collective-permute-start(bf16[128,1600]{1,0:T(8,128)(2,1)S(1)} %add_convert_fusion.1), channel_id=1, source_target_pairs={{1,0},{2,1},{3,2},{0,3},{5,4},{6,5},{7,6},{4,7},{9,8},{10,9},{11,1... | collective-permute-start | bytes 1228808 | tf_op jit(solution)/shard_map/ppermute | solution.py:583
  149.5 21.4 %collective-permute-start.23 = (bf16[128,1600]{1,0:T(8,128)(2,1)S(1)}, bf16[128,1600]{1,0:T(8,128)(2,1)S(1)}, u32[]{:S(2)}, u32[]{:S(2)}) collective-permute-start(bf16[128,1600]{1,0:T(8,128)(2,1)S(1)} %add_convert_fusion.1), channel_id=1, source_target_pairs={{3,0},{0,1},{1,2},{2,3},{7,4},{4,5},{5,6},{6,7},{11,8},{8,9},{9,10... | collective-permute-start | bytes 1228808 | tf_op jit(solution)/shard_map/ppermute | solution.py:583
  185.5 21.4 %collective-permute-start.24 = (bf16[128,1600]{1,0:T(8,128)(2,1)}, bf16[128,1600]{1,0:T(8,128)(2,1)S(1)}, u32[]{:S(2)}, u32[]{:S(2)}) collective-permute-start(bf16[128,1600]{1,0:T(8,128)(2,1)} %get-tuple-element.95), channel_id=1, source_target_pairs={{3,0},{0,1},{1,2},{2,3},{7,4},{4,5},{5,6},{6,7},{11,8},{8,9},{9,10... | collective-permute-start | bytes 1228808 | tf_op jit(solution)/shard_map/ppermute | solution.py:583
  185.5 30.1 %collective-permute-start.25 = (bf16[128,1600]{1,0:T(8,128)(2,1)}, bf16[128,1600]{1,0:T(8,128)(2,1)S(1)}, u32[]{:S(2)}, u32[]{:S(2)}) collective-permute-start(bf16[128,1600]{1,0:T(8,128)(2,1)} %get-tuple-element.96), channel_id=1, source_target_pairs={{2,0},{3,1},{0,2},{1,3},{6,4},{7,5},{4,6},{5,7},{10,8},{11,9},{8,1... | collective-permute-start | bytes 1228808 | tf_op jit(solution)/shard_map/ppermute | solution.py:583
  186.6 29.1 %collective-permute-start.26 = (bf16[128,1600]{1,0:T(8,128)(2,1)S(1)}, bf16[128,1600]{1,0:T(8,128)(2,1)S(1)}, u32[]{:S(2)}, u32[]{:S(2)}) collective-permute-start(bf16[128,1600]{1,0:T(8,128)(2,1)S(1)} %get-tuple-element.97), channel_id=1, source_target_pairs={{1,0},{2,1},{3,2},{0,3},{5,4},{6,5},{7,6},{4,7},{9,8},{10,9},{11,1... | collective-permute-start | bytes 1228808 | tf_op jit(solution)/shard_map/ppermute | solution.py:583
  222.8 24.8 %collective-permute-start.27 = (bf16[128,1600]{1,0:T(8,128)(2,1)S(1)}, bf16[128,1600]{1,0:T(8,128)(2,1)}, u32[]{:S(2)}, u32[]{:S(2)}) collective-permute-start(bf16[128,1600]{1,0:T(8,128)(2,1)S(1)} %get-tuple-element.105), channel_id=1, source_target_pairs={{1,0},{2,1},{3,2},{0,3},{5,4},{6,5},{7,6},{4,7},{9,8},{10,9},{11,1... | collective-permute-start | bytes 1228808 | tf_op jit(solution)/shard_map/ppermute | solution.py:583
  222.9 25.8 %collective-permute-start.28 = (bf16[128,1600]{1,0:T(8,128)(2,1)S(1)}, bf16[128,1600]{1,0:T(8,128)(2,1)S(1)}, u32[]{:S(2)}, u32[]{:S(2)}) collective-permute-start(bf16[128,1600]{1,0:T(8,128)(2,1)S(1)} %get-tuple-element.105), channel_id=1, source_target_pairs={{2,0},{3,1},{0,2},{1,3},{6,4},{7,5},{4,6},{5,7},{10,8},{11,9},{8,1... | collective-permute-start | bytes 1228808 | tf_op jit(solution)/shard_map/ppermute | solution.py:583
  223.8 15.8 %collective-permute-start.35 = (bf16[400,128]{1,0:T(8,128)(2,1)}, bf16[400,128]{1,0:T(8,128)(2,1)}, u32[]{:S(2)}, u32[]{:S(2)}) collective-permute-start(bf16[400,128]{1,0:T(8,128)(2,1)} %get-tuple-element.167), channel_id=1, source_target_pairs={{3,0},{0,1},{1,2},{2,3},{7,4},{4,5},{5,6},{6,7},{11,8},{8,9},{9,10... | collective-permute-start | bytes 307208 | tf_op jit(solution)/shard_map/ppermute | solution.py:583
  225.2 15.9 %collective-permute-start.34 = (bf16[400,128]{1,0:T(8,128)(2,1)}, bf16[400,128]{1,0:T(8,128)(2,1)}, u32[]{:S(2)}, u32[]{:S(2)}) collective-permute-start(bf16[400,128]{1,0:T(8,128)(2,1)} %get-tuple-element.168), channel_id=1, source_target_pairs={{2,0},{3,1},{0,2},{1,3},{6,4},{7,5},{4,6},{5,7},{10,8},{11,9},{8,1... | collective-permute-start | bytes 307208 | tf_op jit(solution)/shard_map/ppermute | solution.py:583
  228.9 17.7 %collective-permute-start.33 = (bf16[400,128]{1,0:T(8,128)(2,1)}, bf16[400,128]{1,0:T(8,128)(2,1)}, u32[]{:S(2)}, u32[]{:S(2)}) collective-permute-start(bf16[400,128]{1,0:T(8,128)(2,1)} %get-tuple-element.169), channel_id=1, source_target_pairs={{1,0},{2,1},{3,2},{0,3},{5,4},{6,5},{7,6},{4,7},{9,8},{10,9},{11,1... | collective-permute-start | bytes 307208 | tf_op jit(solution)/shard_map/ppermute | solution.py:583
  229.9 24.1 %all-to-all-start.1 = ((bf16[32,64,128]{2,1,0:T(8,128)(2,1)}), bf16[32,64,128]{2,1,0:T(8,128)(2,1)S(1)}, u32[]{:S(2)}, u32[]{:S(2)}) async-start(bf16[32,64,128]{2,1,0:T(8,128)(2,1)} %bitcast.95), calls=%async_computation.1 | async-start | bytes 1048576 | tf_op jit(solution)/shard_map/all_to_all | solution.py:683
  254.0 50.4 %all-to-all-start.4 = ((bf16[32,16,1600]{2,1,0:T(8,128)(2,1)}), bf16[32,16,1600]{2,1,0:T(8,128)(2,1)S(1)}, u32[]{:S(2)}, u32[]{:S(2)}) async-start(bf16[32,16,1600]{2,1,0:T(8,128)(2,1)} %out_grad.1), calls=%async_computation.4 | async-start | bytes 3407872 | tf_op jit(solution)/shard_map/all_to_all | solution.py:702
  262.4 25.6 %collective-permute-start.32 = (bf16[128,1600]{1,0:T(8,128)(2,1)}, bf16[128,1600]{1,0:T(8,128)(2,1)S(1)}, u32[]{:S(2)}, u32[]{:S(2)}) collective-permute-start(bf16[128,1600]{1,0:T(8,128)(2,1)} %get-tuple-element.108), channel_id=1, source_target_pairs={{1,0},{2,1},{3,2},{0,3},{5,4},{6,5},{7,6},{4,7},{9,8},{10,9},{11,1... | collective-permute-start | bytes 1228808 | tf_op jit(solution)/shard_map/ppermute | solution.py:583
  262.5 25.6 %collective-permute-start.31 = (bf16[128,1600]{1,0:T(8,128)(2,1)}, bf16[128,1600]{1,0:T(8,128)(2,1)S(1)}, u32[]{:S(2)}, u32[]{:S(2)}) collective-permute-start(bf16[128,1600]{1,0:T(8,128)(2,1)} %get-tuple-element.107), channel_id=1, source_target_pairs={{2,0},{3,1},{0,2},{1,3},{6,4},{7,5},{4,6},{5,7},{10,8},{11,9},{8,1... | collective-permute-start | bytes 1228808 | tf_op jit(solution)/shard_map/ppermute | solution.py:583
  264.5 23.5 %collective-permute-start.30 = (bf16[128,1600]{1,0:T(8,128)(2,1)}, bf16[128,1600]{1,0:T(8,128)(2,1)S(1)}, u32[]{:S(2)}, u32[]{:S(2)}) collective-permute-start(bf16[128,1600]{1,0:T(8,128)(2,1)} %get-tuple-element.106), channel_id=1, source_target_pairs={{3,0},{0,1},{1,2},{2,3},{7,4},{4,5},{5,6},{6,7},{11,8},{8,9},{9,10... | collective-permute-start | bytes 1228808 | tf_op jit(solution)/shard_map/ppermute | solution.py:583
  304.4 75.4 %all-to-all-start.2 = ((bf16[32,192,128]{2,1,0:T(8,128)(2,1)}), bf16[32,192,128]{2,1,0:T(8,128)(2,1)S(1)}, u32[]{:S(2)}, u32[]{:S(2)}) async-start(bf16[32,192,128]{2,1,0:T(8,128)(2,1)} %get-tuple-element.114.grad_ref), calls=%async_computation.2 | async-start | bytes 3145728 | tf_op jit(solution)/shard_map/all_to_all | solution.py:705
  319.1 18.6 %collective-permute-start.42 = (bf16[416,128]{1,0:T(8,128)(2,1)S(1)}, bf16[416,128]{1,0:T(8,128)(2,1)S(1)}, u32[]{:S(2)}, u32[]{:S(2)}) collective-permute-start(bf16[416,128]{1,0:T(8,128)(2,1)S(1)} %get-tuple-element.124), channel_id=1, source_target_pairs={{8,0},{16,8},{24,16},{0,24},{9,1},{17,9},{25,17},{1,25},{10,2},{18... | collective-permute-start | bytes 319496 | tf_op jit(solution)/shard_map/ppermute | solution.py:583
  321.7 17.6 %collective-permute-start.43 = (bf16[416,128]{1,0:T(8,128)(2,1)S(1)}, bf16[416,128]{1,0:T(8,128)(2,1)S(1)}, u32[]{:S(2)}, u32[]{:S(2)}) collective-permute-start(bf16[416,128]{1,0:T(8,128)(2,1)S(1)} %get-tuple-element.124), channel_id=1, source_target_pairs={{16,0},{24,8},{0,16},{8,24},{17,1},{25,9},{1,17},{9,25},{18,2},{26... | collective-permute-start | bytes 319496 | tf_op jit(solution)/shard_map/ppermute | solution.py:583
  322.3 18.8 %collective-permute-start.44 = (bf16[416,128]{1,0:T(8,128)(2,1)S(1)}, bf16[416,128]{1,0:T(8,128)(2,1)S(1)}, u32[]{:S(2)}, u32[]{:S(2)}) collective-permute-start(bf16[416,128]{1,0:T(8,128)(2,1)S(1)} %get-tuple-element.124), channel_id=1, source_target_pairs={{24,0},{0,8},{8,16},{16,24},{25,1},{1,9},{9,17},{17,25},{26,2},{2,... | collective-permute-start | bytes 319496 | tf_op jit(solution)/shard_map/ppermute | solution.py:583
  324.2 20.7 %collective-permute-start.49 = (bf16[416,128]{1,0:T(8,128)(2,1)S(1)}, bf16[416,128]{1,0:T(8,128)(2,1)S(1)}, u32[]{:S(2)}, u32[]{:S(2)}) collective-permute-start(bf16[416,128]{1,0:T(8,128)(2,1)S(1)} %get-tuple-element.126), channel_id=1, source_target_pairs={{32,0},{64,32},{96,64},{0,96},{33,1},{65,33},{97,65},{1,97},{34,2}... | collective-permute-start | bytes 319496 | tf_op jit(solution)/shard_map/ppermute | solution.py:583
  326.7 18.1 %collective-permute-start.50 = (bf16[416,128]{1,0:T(8,128)(2,1)S(1)}, bf16[416,128]{1,0:T(8,128)(2,1)S(1)}, u32[]{:S(2)}, u32[]{:S(2)}) collective-permute-start(bf16[416,128]{1,0:T(8,128)(2,1)S(1)} %get-tuple-element.126), channel_id=1, source_target_pairs={{64,0},{96,32},{0,64},{32,96},{65,1},{97,33},{1,65},{33,97},{66,2}... | collective-permute-start | bytes 319496 | tf_op jit(solution)/shard_map/ppermute | solution.py:583
  344.8 25.2 %collective-permute-start.47 = (bf16[4,416,128]{2,1,0:T(8,128)(2,1)S(1)}, bf16[4,416,128]{2,1,0:T(8,128)(2,1)S(1)}, u32[]{:S(2)}, u32[]{:S(2)}) collective-permute-start(bf16[4,416,128]{2,1,0:T(8,128)(2,1)S(1)} %pad_maximum_fusion), channel_id=1, source_target_pairs={{96,0},{0,32},{32,64},{64,96},{97,1},{1,33},{33,65},{65,97},{98,2}... | collective-permute-start | bytes 1277960 | tf_op jit(solution)/shard_map/ppermute | solution.py:583
  344.9 26.4 %collective-permute-start.52 = (bf16[4,416,128]{2,1,0:T(8,128)(2,1)S(1)}, bf16[4,416,128]{2,1,0:T(8,128)(2,1)S(1)}, u32[]{:S(2)}, u32[]{:S(2)}) collective-permute-start(bf16[4,416,128]{2,1,0:T(8,128)(2,1)S(1)} %pad_maximum_fusion.1), channel_id=1, source_target_pairs={{8,0},{16,8},{24,16},{0,24},{9,1},{17,9},{25,17},{1,25},{10,2},{18... | collective-permute-start | bytes 1277960 | tf_op jit(solution)/shard_map/ppermute | solution.py:583
  347.8 24.3 %collective-permute-start.53 = (bf16[4,416,128]{2,1,0:T(8,128)(2,1)S(1)}, bf16[4,416,128]{2,1,0:T(8,128)(2,1)S(1)}, u32[]{:S(2)}, u32[]{:S(2)}) collective-permute-start(bf16[4,416,128]{2,1,0:T(8,128)(2,1)S(1)} %pad_maximum_fusion.1), channel_id=1, source_target_pairs={{16,0},{24,8},{0,16},{8,24},{17,1},{25,9},{1,17},{9,25},{18,2},{26... | collective-permute-start | bytes 1277960 | tf_op jit(solution)/shard_map/ppermute | solution.py:583
  352.6 20.3 %collective-permute-start.54 = (bf16[4,416,128]{2,1,0:T(8,128)(2,1)S(1)}, bf16[4,416,128]{2,1,0:T(8,128)(2,1)S(1)}, u32[]{:S(2)}, u32[]{:S(2)}) collective-permute-start(bf16[4,416,128]{2,1,0:T(8,128)(2,1)S(1)} %pad_maximum_fusion.1), channel_id=1, source_target_pairs={{24,0},{0,8},{8,16},{16,24},{25,1},{1,9},{9,17},{17,25},{26,2},{2,... | collective-permute-start | bytes 1277960 | tf_op jit(solution)/shard_map/ppermute | solution.py:583
  370.8 45.1 %collective-permute-start.48 = (bf16[16,416,128]{2,1,0:T(8,128)(2,1)}, bf16[16,416,128]{2,1,0:T(8,128)(2,1)}, u32[]{:S(2)}, u32[]{:S(2)}) collective-permute-start(bf16[16,416,128]{2,1,0:T(8,128)(2,1)} %constant_dynamic-update-slice_fusion.20.left_own), channel_id=1, source_target_pairs={{4,0},{0,4},{5,1},{1,5},{6,2},{2,6},{7,3},{3,7},{12,8},{8,12},{13,... | collective-permute-start | bytes 5111816 | tf_op jit(solution)/shard_map/ppermute | solution.py:583
  373.7 42.2 %collective-permute-start.55 = (bf16[16,416,128]{2,1,0:T(8,128)(2,1)}, bf16[16,416,128]{2,1,0:T(8,128)(2,1)}, u32[]{:S(2)}, u32[]{:S(2)}) collective-permute-start(bf16[16,416,128]{2,1,0:T(8,128)(2,1)} %constant_dynamic-update-slice_fusion.27.right_own), channel_id=1, source_target_pairs={{4,0},{0,4},{5,1},{1,5},{6,2},{2,6},{7,3},{3,7},{12,8},{8,12},{13,... | collective-permute-start | bytes 5111816 | tf_op jit(solution)/shard_map/ppermute | solution.py:583
  395.5 19.8 %all-to-all-start.3 = ((f32[32,8,400]{2,1,0:T(8,128)}), f32[32,8,400]{2,1,0:T(8,128)S(1)}, u32[]{:S(2)}, u32[]{:S(2)}) async-start(f32[32,8,400]{2,1,0:T(8,128)} %broadcast_in_dim.29), calls=%async_computation.3 | async-start | bytes 1048576 | tf_op jit(solution)/shard_map/all_to_all | solution.py:730
  406.7 32.5 %collective-permute-start.56 = (bf16[208,1600]{1,0:T(8,128)(2,1)}, bf16[208,1600]{1,0:T(8,128)(2,1)S(1)}, u32[]{:S(2)}, u32[]{:S(2)}) collective-permute-start(bf16[208,1600]{1,0:T(8,128)(2,1)} %get-tuple-element.154), channel_id=1, source_target_pairs={{1,0},{2,1},{3,2},{0,3},{5,4},{6,5},{7,6},{4,7},{9,8},{10,9},{11,1... | collective-permute-start | bytes 1996808 | tf_op jit(solution)/shard_map/ppermute | solution.py:583
  409.4 30.9 %collective-permute-start.58 = (bf16[208,1600]{1,0:T(8,128)(2,1)}, bf16[208,1600]{1,0:T(8,128)(2,1)S(1)}, u32[]{:S(2)}, u32[]{:S(2)}) collective-permute-start(bf16[208,1600]{1,0:T(8,128)(2,1)} %get-tuple-element.153), channel_id=1, source_target_pairs={{2,0},{3,1},{0,2},{1,3},{6,4},{7,5},{4,6},{5,7},{10,8},{11,9},{8,1... | collective-permute-start | bytes 1996808 | tf_op jit(solution)/shard_map/ppermute | solution.py:583
  410.1 33.3 %collective-permute-start.60 = (bf16[208,1600]{1,0:T(8,128)(2,1)S(1)}, bf16[208,1600]{1,0:T(8,128)(2,1)S(1)}, u32[]{:S(2)}, u32[]{:S(2)}) collective-permute-start(bf16[208,1600]{1,0:T(8,128)(2,1)S(1)} %get-tuple-element.152), channel_id=1, source_target_pairs={{3,0},{0,1},{1,2},{2,3},{7,4},{4,5},{5,6},{6,7},{11,8},{8,9},{9,10... | collective-permute-start | bytes 1996808 | tf_op jit(solution)/shard_map/ppermute | solution.py:583
  (61 other events, 610.1 us)
Sparse Core Ops, SparseCore 0:
  10.3 68.9 all-gather.2
  81.5 86.2 all-gather.4
  229.2 168.0 all-reduce.4
